TPU v7x, 128 devices: a whole 4x4x4 slice. The times are simulated.
128 devices in a mesh: blk: 32 (over z, x_hi, y), col: 4 (over x_lo, core).
Axes of the slice: x: 4 (x_hi: 2, x_lo: 2; x = x_hi * 2 + x_lo), y: 4, z: 4, core: 2. Of those that a mesh axis runs over, the one named last changes fastest.
Arguments:
- worker_emb: float32 [65536, 256], P('blk', 'col'), may hold values from -24 to 24
- job_emb: float32 [8192, 256], P('blk', 'col'), may hold values from -48 to 48
- worker_cot: float32 [65536, 256], P('blk', 'col'), may hold values from -24 to 24
- job_cot: float32 [8192, 256], P('blk', 'col'), may hold values from -48 to 48
- worker_deg: int32 [65536], P('blk'), may hold values from 1 to 65568, as said below
- job_deg: int32 [8192], P('blk'), may hold values from 1 to 2097184, as said below
- block_rows: int32 [16384], P(('blk', 'col')), may hold values from 0 to 15, as said below
- block_cols: int32 [16384], P(('blk', 'col')), may hold values from 0 to 63
- block_tiles: int32 [16384, 128, 128], P(('blk', 'col')), may hold values from 0 to 1
- live_count: int32 [32, 4], P('blk', 'col'), may hold values from 16 to 128, as said below
Outputs:
- worker_out: float32 [65536, 256], P('blk', 'col')
- job_out: float32 [8192, 256], P('blk', 'col')
- worker_grad: float32 [65536, 256], P('blk', 'col')
- job_grad: float32 [8192, 256], P('blk', 'col')
Inputs may be any that keep to these rules, and one draw needn't show every extreme that they name: `block_rows`: worker block row within the 16 row blocks of the slot's blk index. `live_count`: slots from this count on are ignored; some device has all 128 slots live. `worker_deg`: at least the worker's number of edges in A. `job_deg`: at least the job's number of edges in A.
All inputs are finite; a program needn't handle non-finite values.
Results may differ from a plain program's by a relative error of at most 0.0029.
Values may be sent and summed in bfloat16 or wider, within the bound.
A program may use at most 128 MiB of HBM per device.

v0:
```python
import jax
import jax.numpy as jnp
from jax import lax
from jax.sharding import PartitionSpec as P


def on_device(
    worker_emb,
    job_emb,
    worker_cot,
    job_cot,
    worker_deg,
    job_deg,
    block_rows,
    block_cols,
    block_tiles,
    live_count,
):
    tile_size = block_tiles.shape[1]
    slot_count = block_tiles.shape[0]
    quarter = worker_emb.shape[1]
    worker_scale = lax.rsqrt(worker_deg.astype(jnp.float32))[:, None]
    job_scale = lax.rsqrt(job_deg.astype(jnp.float32))[:, None]
    worker_src = jnp.concatenate(
        [worker_emb * worker_scale, worker_cot * worker_scale], axis=1
    ).astype(jnp.bfloat16)
    job_src = jnp.concatenate([job_emb * job_scale, job_cot * job_scale], axis=1).astype(
        jnp.bfloat16
    )
    worker_full, job_full = (
        lax.all_gather(worker_src, "col", axis=1, tiled=True),
        lax.all_gather(job_src, "col", axis=1, tiled=True),
    )
    job_table = lax.all_gather(job_full, "blk", axis=0, tiled=True)
    width = job_table.shape[1]
    live_mask = jnp.arange(slot_count) < live_count[0, 0]
    dense = jnp.where(live_mask[:, None, None], block_tiles, 0).astype(jnp.bfloat16)
    job_blocks = job_table.reshape(-1, tile_size, width)[block_cols]
    forward = jnp.einsum("sij,sjk->sik", dense, job_blocks, preferred_element_type=jnp.float32)
    row_blocks = worker_full.shape[0] // tile_size
    worker_sum = jax.ops.segment_sum(forward, block_rows, num_segments=row_blocks).reshape(
        -1, width
    )
    worker_blocks = worker_full.reshape(row_blocks, tile_size, width)[block_rows]
    flipped = jnp.einsum("sji,sjk->sik", dense, worker_blocks, preferred_element_type=jnp.float32)
    job_block_count = job_table.shape[0] // tile_size
    job_partial = jax.ops.segment_sum(flipped, block_cols, num_segments=job_block_count).reshape(
        -1, width
    )
    job_rows = lax.psum_scatter(job_partial, "blk", scatter_dimension=0, tiled=True)
    worker_part, job_part = (
        lax.psum_scatter(worker_sum, "col", scatter_dimension=1, tiled=True),
        lax.psum_scatter(job_rows, "col", scatter_dimension=1, tiled=True),
    )
    worker_out = worker_scale * worker_part[:, :quarter]
    worker_grad = worker_scale * worker_part[:, quarter:]
    job_out = job_scale * job_part[:, :quarter]
    job_grad = job_scale * job_part[:, quarter:]
    return (worker_out, job_out, worker_grad, job_grad)


def solution(mesh):
    return jax.shard_map(
        on_device,
        mesh=mesh,
        in_specs=(
            P("blk", "col"),
            P("blk", "col"),
            P("blk", "col"),
            P("blk", "col"),
            P("blk"),
            P("blk"),
            P(("blk", "col")),
            P(("blk", "col")),
            P(("blk", "col"), None, None),
            P("blk", "col"),
        ),
        out_specs=(P("blk", "col"), P("blk", "col"), P("blk", "col"), P("blk", "col")),
        check_vma=False,
    )
```

profile of v0, /device:TPU:0, one launch (start us, length us, event | category | flops | bytes accessed | tf_op | source)
XLA Modules:
  0.0 701.6 jit_solution(3491363497995628790)
XLA Ops:
  7.2 0.0 all-gather.3.cloned.1.call-start
  7.2 0.7 convert_rsqrt_fusion.1
  7.9 0.9 multiply_convert_fusion.3
  8.8 6.3 all_gather.9
  15.1 0.0 all-gather.3.cloned.1.call-update
  15.1 0.0 reduce-scatter.4.cloned.1.call-start
  15.8 0.7 compare_select_fusion.1
  16.5 101.5 %all-gather.3.cloned.1.call-done = bf16[8192,512]{0,1:T(8,128)(2,1)} async-done(((bf16[256,512]{0,1:T(8,128)(2,1)}), bf16[8192,512]{0,1:T(8,128)(2,1)}) %all-gather.3.cloned.1.call-update) | async-done | bytes 8388624 | tf_op jit(solution)/shard_map/all_gather | solution.py:34
  118.0 11.9 %copy.15 = bf16[8192,512]{1,0:T(8,128)(2,1)} copy(bf16[8192,512]{0,1:T(8,128)(2,1)} %all-gather.3.cloned.1.call-done) | data formatting | bytes 16777216 | tf_op jit(solution)/shard_map/all_gather | solution.py:34
  129.9 11.8 %gather_fusion = bf16[128,128,512]{2,1,0:T(8,128)(2,1)} fusion(bf16[64,128,512]{2,1,0:T(8,128)(2,1)} %bitcast.11, s32[1024]{0:T(1024)S(1)} %pad_clamp_fusion.1), kind=kCustom, calls=%fused_computation | custom fusion | bytes 33554944 | tf_op jit(solution)/shard_map/gather | solution.py:38
  141.7 0.0 copy-start.3
  141.7 20.1 %fusion.1 = f32[128,128,512]{2,1,0:T(8,128)} fusion(bf16[128,128,512]{2,1,0:T(8,128)(2,1)} %gather_fusion, s32[128,128,128]{2,1,0:T(8,128)} %param.18, pred[128]{0:T(512)(128)(4,1)S(1)} %iota_compare_fusion), kind=kOutput, calls=%fused_computation.23 | convolution fusion | flops 2151677952 | bytes 58720384 | tf_op jit(solution)/shard_map/sij,sjk->sik/dot_general | solution.py:39
  161.8 2.6 broadcast_in_dim.33
  164.4 0.0 copy-done.3
  164.4 0.0 copy-start.2
  164.4 0.0 copy-start
  164.4 0.0 copy-start.1
  164.4 72.4 %scatter_fusion = f32[16,128,512]{2,1,0:T(8,128)} fusion(f32[16,128,512]{2,1,0:T(8,128)} %broadcast_in_dim.33, s32[128]{0:T(128)S(1)} %copy-done.3, f32[128,128,512]{2,1,0:T(8,128)} %fusion.1), kind=kCustom, calls=%fused_computation.2 | custom fusion | flops 8388608 | bytes 100663808 | tf_op jit(solution)/shard_map/scatter-add | solution.py:41
  236.8 5.4 copy.16
  242.2 0.0 reduce-scatter.4.cloned.1.call-update
  242.2 0.0 all-gather.5.cloned.1.call-start
  242.3 0.0 copy-done.2
  242.3 44.2 %reduce-scatter.4.cloned.1.call-done = f32[2048,128]{0,1:T(8,128)} async-done(((f32[2048,512]{0,1:T(8,128)}), f32[2048,128]{0,1:T(8,128)}) %reduce-scatter.4.cloned.1.call-update) | async-done | bytes 1048592 | tf_op jit(solution)/shard_map/reduce_scatter | solution.py:52
  286.5 0.0 copy-done
  286.5 0.0 copy-done.1
  286.5 2.3 slice_multiply_fusion
  288.8 0.9 pad_maximum_fusion
  289.7 0.0 all-gather.5.cloned.1.call-update
  289.7 0.0 reduce-scatter.6.cloned.1.call-start
  289.8 30.0 %all-gather.5.cloned.1.call-done = bf16[2048,512]{0,1:T(8,128)(2,1)} async-done(((bf16[2048,128]{0,1:T(8,128)(2,1)}), bf16[2048,512]{0,1:T(8,128)(2,1)}) %all-gather.5.cloned.1.call-update) | async-done | bytes 2097168 | tf_op jit(solution)/shard_map/all_gather | solution.py:31
  319.7 2.9 copy.17
  322.6 8.4 %gather_fusion.1 = bf16[128,128,512]{2,1,0:T(8,128)(2,1)} fusion(bf16[16,128,512]{2,1,0:T(8,128)(2,1)S(1)} %bitcast.10, s32[1024]{0:T(1024)S(1)} %pad_clamp_fusion), kind=kCustom, calls=%fused_computation.1 | custom fusion | bytes 33554944 | tf_op jit(solution)/shard_map/gather | solution.py:44
  331.0 20.2 %fusion = f32[128,128,512]{2,1,0:T(8,128)} fusion(bf16[128,128,512]{2,1,0:T(8,128)(2,1)} %gather_fusion.1, s32[128,128,128]{2,1,0:T(8,128)} %param.18, pred[128]{0:T(512)(128)(4,1)S(1)} %iota_compare_fusion), kind=kOutput, calls=%fused_computation.22 | convolution fusion | flops 2151677952 | bytes 58720384 | tf_op jit(solution)/shard_map/sji,sjk->sik/dot_general | solution.py:45
  351.3 0.0 copy-start.4
  351.3 7.9 %broadcast_in_dim.38 = f32[64,128,512]{2,1,0:T(8,128)} broadcast(f32[]{:T(128)} %constant.4.clone.1), dimensions={} | broadcast | bytes 16777220 | tf_op jit(solution)/shard_map/broadcast_in_dim | solution.py:47
  359.1 0.0 copy-done.4
  359.1 73.2 %scatter_fusion.1 = f32[64,128,512]{2,1,0:T(8,128)} fusion(f32[64,128,512]{2,1,0:T(8,128)} %broadcast_in_dim.38, s32[128]{0:T(128)S(1)} %copy-done.4, f32[128,128,512]{2,1,0:T(8,128)} %fusion), kind=kCustom, calls=%fused_computation.3 | custom fusion | flops 8388608 | bytes 100663808 | tf_op jit(solution)/shard_map/scatter-add | solution.py:47
  432.3 17.4 %copy.19 = f32[8192,512]{0,1:T(8,128)} copy(f32[8192,512]{1,0:T(8,128)} %bitcast.9) | data formatting | bytes 33554432 | tf_op jit(solution)/shard_map/reshape | solution.py:47
  449.8 0.0 reduce-scatter.6.cloned.1.call-update
  449.8 0.0 reduce-scatter.8.cloned.1.call-start
  449.8 225.6 %reduce-scatter.6.cloned.1.call-done = f32[256,512]{0,1:T(8,128)} async-done(((f32[8192,512]{0,1:T(8,128)}), f32[256,512]{0,1:T(8,128)}) %reduce-scatter.6.cloned.1.call-update) | async-done | bytes 524304 | tf_op jit(solution)/shard_map/reduce_scatter | solution.py:50
  675.4 0.0 reduce-scatter.8.cloned.1.call-update
  675.5 18.0 %reduce-scatter.8.cloned.1.call-done = f32[256,128]{0,1:T(8,128)} async-done(((f32[256,512]{0,1:T(8,128)}), f32[256,128]{0,1:T(8,128)}) %reduce-scatter.8.cloned.1.call-update) | async-done | bytes 131088 | tf_op jit(solution)/shard_map/reduce_scatter | solution.py:53
  693.5 1.5 slice_multiply_fusion.2
  (6 shorter events, 0.0 us)
Async XLA Ops:
  7.2 110.8 %all-gather.3.cloned.1.call-start = ((), (), s32[]{:S(2)}) async-start(), calls=%async_computation.3 | async-start | bytes 8650752 | tf_op jit(solution)/shard_map/all_gather | solution.py:34
  15.1 271.4 %reduce-scatter.4.cloned.1.call-start = ((), (), s32[]{:S(2)}) async-start(), calls=%async_computation.4 | async-start | bytes 5242880 | tf_op jit(solution)/shard_map/reduce_scatter | solution.py:52
  141.7 22.7 %copy-start.3 = (s32[128]{0:T(128)S(1)}, s32[128]{0:T(128)}, u32[]{:S(2)}) copy-start(s32[128]{0:T(128)} %param.16) | copy-start | bytes 1540
  164.4 77.9 %copy-start.2 = (s32[2048]{0:T(1024)S(1)}, s32[2048]{0:T(1024)}, u32[]{:S(2)}) copy-start(s32[2048]{0:T(1024)} %param.14) | copy-start | bytes 24580
  164.4 122.1 %copy-start = (f32[2048,64]{0,1:T(8,128)S(1)}, f32[2048,64]{0,1:T(8,128)}, u32[]{:S(2)}) copy-start(f32[2048,64]{0,1:T(8,128)} %param.10) | copy-start | bytes 1572868
  164.4 122.1 %copy-start.1 = (f32[2048,64]{0,1:T(8,128)S(1)}, f32[2048,64]{0,1:T(8,128)}, u32[]{:S(2)}) copy-start(f32[2048,64]{0,1:T(8,128)} %param.12) | copy-start | bytes 1572868
  242.2 77.5 %all-gather.5.cloned.1.call-start = ((), (), s32[]{:S(2)}) async-start(), calls=%async_computation.5 | async-start | bytes 2621440 | tf_op jit(solution)/shard_map/all_gather | solution.py:31
  289.7 385.8 %reduce-scatter.6.cloned.1.call-start = ((), (), s32[]{:S(2)}) async-start(), calls=%async_computation.6 | async-start | bytes 17301504 | tf_op jit(solution)/shard_map/reduce_scatter | solution.py:50
  351.3 7.9 %copy-start.4 = (s32[128]{0:T(128)S(1)}, s32[128]{0:T(128)}, u32[]{:S(2)}) copy-start(s32[128]{0:T(128)} %param.17) | copy-start | bytes 1540
  449.8 243.7 %reduce-scatter.8.cloned.1.call-start = ((), (), s32[]{:S(2)}) async-start(), calls=%async_computation.7 | async-start | bytes 655360 | tf_op jit(solution)/shard_map/reduce_scatter | solution.py:53
Sparse Core Ops, SparseCore 0:
  15.2 102.7 all-gather.2
  242.3 44.0 reduce-scatter.3
  289.8 29.8 all-gather.4
  449.9 225.4 reduce-scatter.5
  677.8 15.6 reduce-scatter.7
where the time goes:
time: 705 us; the launch traced here: 702 us
  waiting for transfers between devices  419 us (59%)
  other arithmetic  153 us (22%)
  local copies, waits for them, and re-layouts  68.4 us (10%)
  matrix products  40.3 us (6%)
  between operations  14.5 us (2%)
    reduce_scatter x1, waiting for transfers between devices, on_device(): lax.psum_scatter(job_partial, 'blk', scatter_dimension=0, tiled=True)  226 us
    all_gather x1, waiting for transfers between devices, on_device(): job_table = lax.all_gather(job_full, 'blk', axis=0, tiled=True)  101 us
    scatter-add x1, other arithmetic, on_device(): jax.ops.segment_sum(flipped, block_cols, num_segments=job_block_count)  73.2 us
    scatter-add x1, other arithmetic, on_device(): jax.ops.segment_sum(forward, block_rows, num_segments=row_blocks)  72.4 us
    reduce_scatter x1, waiting for transfers between devices, on_device(): lax.psum_scatter(worker_sum, 'col', scatter_dimension=1, tiled=True)  44.2 us
    all_gather x1, waiting for transfers between devices, on_device(): lax.all_gather(worker_src, 'col', axis=1, tiled=True)  30 us
    dot_general x1, matrix products, on_device(): jnp.einsum('sji,sjk->sik', dense, worker_blocks, preferred_element_type=j...  20.2 us
    dot_general x1, matrix products, on_device(): jnp.einsum('sij,sjk->sik', dense, job_blocks, preferred_element_type=jnp....  20.1 us
  transfers between devices with their start and end apart: 5, of which 5 were waited for; matrix products, arithmetic and copies ran while one was open for 0% of the time, Pallas kernels for 0%

commit v1 on v0

v1 whole, which is shorter than its diff:
```python
import functools

import jax
import jax.numpy as jnp
from jax import lax
from jax.experimental import pallas as pl
from jax.experimental.pallas import tpu as pltpu
from jax.sharding import PartitionSpec as P

MESH = pl.DeviceIdType.MESH
TILE = 128
NB = 128
RB = 16
NJB = 64
NW_LOC = RB * TILE
NJ = NJB * TILE
JLOC = 256
PARTS = ((0, 96, "xyz"), (96, 80, "yzx"), (176, 80, "zxy"))
DIMS = (("x", 2), ("z", 4), ("x", 2), ("y", 4))
TCHUNK = 8
NCHUNK = NB // TCHUNK
NBUF = 4
KCHUNK = 32
GROUP = 16


def position():
    blk = lax.axis_index("blk")
    col = lax.axis_index("col")
    return {
        "z": blk // 8,
        "x": ((blk // 4) % 2) * 2 + col // 2,
        "y": blk % 4,
        "core": col % 2,
    }


def device(at):
    x = at["x"]
    return (at["z"] * 8 + (x // 2) * 4 + at["y"], (x % 2) * 2 + at["core"])


def shifted(at, axis, by):
    return {**at, axis: (at[axis] + by + 4) % 4}


def neighbours(at):
    out = [device(shifted(at, axis, d)) for axis in "xyz" for d in (1, 2, 3)]
    out.append(device({**at, "core": 1 - at["core"]}))
    return out


def greet(at):
    barrier = pltpu.get_barrier_semaphore()
    others = neighbours(at)
    for other in others:
        pl.semaphore_signal(barrier, inc=1, device_id=other, device_id_type=MESH)
    pl.semaphore_wait(barrier, len(others))


def dims_of(axes):
    return tuple(n for name, n in DIMS if name in axes)


def pick(axes, fixed):
    index = []
    seen_x = False
    for name, _ in DIMS:
        if name not in axes:
            continue
        if name not in fixed:
            index.append(slice(None))
        elif name == "x":
            index.append(fixed["x"] // 2 if seen_x else fixed["x"] % 2)
        else:
            index.append(fixed[name])
        if name == "x":
            seen_x = True
    return tuple(index)


def gather_kernel(
    wsrc,
    jsrc,
    tiles,
    meta,
    table,
    workers,
    tiles_out,
    meta_out,
    tin,
    tb,
    tin_sem,
    tsend,
    trecv,
    tlocal,
    gsend,
    grecv,
    osend,
    orecv,
    olocal,
):
    at = position()
    x_lo = at["x"] % 2
    core = at["core"]

    def load(i):
        return pltpu.make_async_copy(
            tiles.at[pl.ds(i * TCHUNK, TCHUNK)], tin.at[i % NBUF], tin_sem.at[i % NBUF]
        )

    for i in range(NBUF):
        load(i).start()
    local = [
        pltpu.make_async_copy(jsrc, table.at[pick("xyz", at)], olocal.at[0]),
        pltpu.make_async_copy(wsrc, workers.at[x_lo], olocal.at[1]),
        pltpu.make_async_copy(meta, meta_out.at[core], olocal.at[2]),
    ]
    for c in local:
        c.start()
    greet(at)

    def remote(src, dst, sems, rems, i, target):
        c = pltpu.make_async_remote_copy(
            src_ref=src,
            dst_ref=dst,
            send_sem=sems.at[i],
            recv_sem=rems.at[i],
            device_id=device(target),
            device_id_type=MESH,
        )
        c.start()
        return c

    def rows(p):
        return pl.ds(PARTS[p][0], PARTS[p][1])

    def piece(p, fixed):
        return table.at[pick("xyz", fixed) + (rows(p), slice(None))]

    first, second, third = {}, {}, {}
    for p in range(3):
        a1, a2, a3 = PARTS[p][2]
        for d in (1, 2, 3):
            first[p, d] = remote(
                jsrc.at[rows(p)], piece(p, at), gsend, grecv, p * 18 + d - 1, shifted(at, a1, d)
            )
    partner = {**at, "core": 1 - core}
    mcopy = remote(meta, meta_out.at[core], osend, orecv, 0, partner)
    wcopy = remote(wsrc, workers.at[x_lo], osend, orecv, 1, {**at, "x": at["x"] + 1 - 2 * x_lo})

    tcopies = []

    def chunk(i):
        load(i).wait()
        tb[pl.ds(i * TCHUNK, TCHUNK)] = tin[i % NBUF].astype(jnp.float32).astype(jnp.bfloat16)
        if i + NBUF < NCHUNK:
            load(i + NBUF).start()
        here = tb.at[pl.ds(i * TCHUNK, TCHUNK)]
        there = tiles_out.at[core, pl.ds(i * TCHUNK, TCHUNK)]
        tcopies.append(remote(here, there, tsend, trecv, i, partner))
        c = pltpu.make_async_copy(here, there, tlocal.at[i])
        c.start()
        local.append(c)

    for i in range(4):
        chunk(i)
    local[0].wait()
    for p in range(3):
        a1, a2, a3 = PARTS[p][2]
        for d in (1, 2, 3):
            first[p, d].wait_recv()
        own = piece(p, {a2: at[a2], a3: at[a3]})
        for d in (1, 2, 3):
            second[p, d] = remote(own, own, gsend, grecv, p * 18 + 3 + d - 1, shifted(at, a2, d))
    for p in range(3):
        a1, a2, a3 = PARTS[p][2]
        own = piece(p, {a2: at[a2], a3: at[a3]})
        for d in (1, 2, 3):
            third[p, 0, d] = remote(own, own, gsend, grecv, p * 18 + 6 + d - 1, shifted(at, a3, d))
    for i in range(4, 8):
        chunk(i)
    for g in (1, 3, 2):
        for p in range(3):
            a1, a2, a3 = PARTS[p][2]
            second[p, g].wait_recv()
            got = piece(p, {a2: (at[a2] - g + 4) % 4, a3: at[a3]})
            for d in (1, 2, 3):
                third[p, g, d] = remote(
                    got, got, gsend, grecv, p * 18 + 6 + g * 3 + d - 1, shifted(at, a3, d)
                )
    for i in range(8, NCHUNK):
        chunk(i)
    for c in local[1:]:
        c.wait()
    mcopy.wait()
    wcopy.wait()
    for c in tcopies:
        c.wait()
    for c in list(first.values()) + list(second.values()):
        c.wait_send()
    for c in third.values():
        c.wait()


def gather(wsrc, jsrc, tiles, meta):
    hbm = pl.BlockSpec(memory_space=pl.ANY)
    return pl.pallas_call(
        gather_kernel,
        in_specs=[hbm] * 4,
        out_specs=[hbm] * 4,
        out_shape=[
            jax.ShapeDtypeStruct(dims_of("xyz") + (JLOC, TILE), jnp.bfloat16),
            jax.ShapeDtypeStruct((2, NW_LOC, TILE), jnp.bfloat16),
            jax.ShapeDtypeStruct((2, NB, TILE, TILE), jnp.bfloat16),
            jax.ShapeDtypeStruct((2, 8, TILE), jnp.int32),
        ],
        scratch_shapes=[
            pltpu.VMEM((NBUF, TCHUNK, TILE, TILE), jnp.int32),
            pltpu.VMEM((NB, TILE, TILE), jnp.bfloat16),
            pltpu.SemaphoreType.DMA((NBUF,)),
            pltpu.SemaphoreType.DMA((NCHUNK,)),
            pltpu.SemaphoreType.DMA((NCHUNK,)),
            pltpu.SemaphoreType.DMA((NCHUNK,)),
            pltpu.SemaphoreType.DMA((54,)),
            pltpu.SemaphoreType.DMA((54,)),
            pltpu.SemaphoreType.DMA((2,)),
            pltpu.SemaphoreType.DMA((2,)),
            pltpu.SemaphoreType.DMA((3,)),
        ],
        compiler_params=pltpu.CompilerParams(
            collective_id=0, has_side_effects=True, vmem_limit_bytes=56 * 2**20
        ),
        name="gather_all",
    )(wsrc, jsrc, tiles, meta)


def sparse_kernel(
    meta, table, workers, tiles, jobs_out, away_out, home_out, tbuf, wbuf, xbuf, jacc, wacc, jbf, abf, sems, tsems, osems
):
    def tile_load(k):
        return pltpu.make_async_copy(
            tiles.at[pl.ds(k * KCHUNK, KCHUNK)], xbuf.at[pl.ds(k * KCHUNK, KCHUNK)], tsems.at[k]
        )

    wload = pltpu.make_async_copy(workers, wbuf, sems.at[0])
    tload = pltpu.make_async_copy(table, tbuf, sems.at[1])
    wload.start()
    tload.start()

    @pl.loop(0, 2 * NB // KCHUNK)
    def _(k):
        tile_load(k).start()

    @pl.loop(0, NJB)
    def _(j):
        jacc[:, pl.ds(j * TILE, TILE), :] = jnp.zeros((2, TILE, TILE), jnp.float32)

    @pl.loop(0, RB)
    def _(j):
        wacc[:, pl.ds(j * TILE, TILE), :] = jnp.zeros((2, TILE, TILE), jnp.float32)

    wload.wait()
    tload.wait()

    @pl.loop(0, 2 * NB // KCHUNK)
    def _(k):
        tile_load(k).wait()
        half = k // (NB // KCHUNK)
        live = meta[half, 2, 0]

        @pl.loop(0, KCHUNK // GROUP)
        def _(q):
            start = (k % (NB // KCHUNK)) * KCHUNK + q * GROUP

            @pl.when(start < live)
            def _():
                for g in range(GROUP):
                    s = start + g
                    r = pl.multiple_of(meta[half, 0, s] * TILE, TILE)
                    c = pl.multiple_of(meta[half, 1, s] * TILE, TILE)
                    tile = xbuf[half * NB + s]
                    tile = jnp.where(s < live, tile, jnp.zeros_like(tile))
                    jb = jnp.concatenate(
                        [tbuf[0, pl.ds(c, TILE), :], tbuf[1, pl.ds(c, TILE), :]], axis=1
                    )
                    f = jnp.dot(tile, jb, preferred_element_type=jnp.float32)
                    wacc[0, pl.ds(r, TILE), :] += f[:, :TILE]
                    wacc[1, pl.ds(r, TILE), :] += f[:, TILE:]
                    wb = jnp.concatenate(
                        [wbuf[0, pl.ds(r, TILE), :], wbuf[1, pl.ds(r, TILE), :]], axis=1
                    )
                    t = lax.dot_general(
                        tile, wb, (((0,), (0,)), ((), ())), preferred_element_type=jnp.float32
                    )
                    jacc[0, pl.ds(c, TILE), :] += t[:, :TILE]
                    jacc[1, pl.ds(c, TILE), :] += t[:, TILE:]

    x_lo = meta[0, 3, 0]

    @pl.loop(0, RB)
    def _(j):
        here = pl.ds(j * TILE, TILE)
        abf[here, :] = wacc[1 - x_lo, here, :].astype(jnp.bfloat16)

    outs = [
        pltpu.make_async_copy(wacc.at[x_lo], home_out, osems.at[0]),
        pltpu.make_async_copy(abf, away_out, osems.at[1]),
    ]
    for c in outs:
        c.start()

    @pl.loop(0, NJB)
    def _(j):
        here = pl.ds(j * TILE, TILE)
        jbf[:, here, :] = jacc[:, here, :].astype(jnp.bfloat16)

    c = pltpu.make_async_copy(jbf, jobs_out, osems.at[2])
    c.start()
    c.wait()
    for c in outs:
        c.wait()


def sparse_products(meta, table, workers, tiles):
    hbm = pl.BlockSpec(memory_space=pl.ANY)
    flops = 2 * 2 * 2 * NB * TILE * TILE * 256
    return pl.pallas_call(
        sparse_kernel,
        grid_spec=pltpu.PrefetchScalarGridSpec(
            num_scalar_prefetch=1,
            grid=(),
            in_specs=[hbm] * 3,
            out_specs=[hbm] * 3,
            scratch_shapes=[
                pltpu.VMEM((2, NJ, TILE), jnp.bfloat16),
                pltpu.VMEM((2, NW_LOC, TILE), jnp.bfloat16),
                pltpu.VMEM((2 * NB, TILE, TILE), jnp.bfloat16),
                pltpu.VMEM((2, NJ, TILE), jnp.float32),
                pltpu.VMEM((2, NW_LOC, TILE), jnp.float32),
                pltpu.VMEM((2, NJ, TILE), jnp.bfloat16),
                pltpu.VMEM((NW_LOC, TILE), jnp.bfloat16),
                pltpu.SemaphoreType.DMA((2,)),
                pltpu.SemaphoreType.DMA((2 * NB // KCHUNK,)),
                pltpu.SemaphoreType.DMA((3,)),
            ],
        ),
        out_shape=[
            jax.ShapeDtypeStruct((2, NJ, TILE), jnp.bfloat16),
            jax.ShapeDtypeStruct((NW_LOC, TILE), jnp.bfloat16),
            jax.ShapeDtypeStruct((NW_LOC, TILE), jnp.float32),
        ],
        compiler_params=pltpu.CompilerParams(vmem_limit_bytes=56 * 2**20),
        cost_estimate=pl.CostEstimate(flops=flops, bytes_accessed=22 * 2**20, transcendentals=0),
        name="sparse_products",
    )(meta, table, workers, tiles)


def scatter_kernel(
    jobs,
    away,
    home,
    jout,
    wout,
    own0,
    own1,
    own2,
    ra0,
    ra1,
    ra2,
    sa0,
    sa1,
    sa2,
    rb0,
    rb1,
    rb2,
    sb0,
    sb1,
    sb2,
    rc0,
    rc1,
    rc2,
    rw,
    lsem,
    wsend,
    wrecv,
    gsend,
    grecv,
):
    own, ra, sa = (own0, own1, own2), (ra0, ra1, ra2), (sa0, sa1, sa2)
    rb, sb, rc = (rb0, rb1, rb2), (sb0, sb1, sb2), (rc0, rc1, rc2)
    at = position()
    x_lo = at["x"] % 2

    def rows(p):
        return pl.ds(PARTS[p][0], PARTS[p][1])

    def remote(src, dst, i, target):
        c = pltpu.make_async_remote_copy(
            src_ref=src,
            dst_ref=dst,
            send_sem=gsend.at[i],
            recv_sem=grecv.at[i],
            device_id=device(target),
            device_id_type=MESH,
        )
        c.start()
        return c

    local = []
    for p in range(3):
        a1 = PARTS[p][2][0]
        c = pltpu.make_async_copy(
            jobs.at[pick("xyz", {a1: at[a1]}) + (rows(p), slice(None))], own[p], lsem.at[p]
        )
        c.start()
        local.append(c)
    greet(at)
    first, second, third = {}, {}, {}
    for d in (2, 1, 3):
        for p in range(3):
            a1 = PARTS[p][2][0]
            target = shifted(at, a1, d)
            first[p, d] = remote(
                jobs.at[pick("xyz", {a1: target[a1]}) + (rows(p), slice(None))],
                ra[p].at[d - 1],
                p * 9 + d - 1,
                target,
            )
    partner = {**at, "x": at["x"] + 1 - 2 * x_lo}
    wcopy = pltpu.make_async_remote_copy(
        src_ref=away,
        dst_ref=rw,
        send_sem=wsend,
        recv_sem=wrecv,
        device_id=device(partner),
        device_id_type=MESH,
    )
    wcopy.start()

    def loop_index(axes, k):
        index = []
        for n in reversed(dims_of(axes)):
            index.append(k % n)
            k = k // n
        return tuple(reversed(index))

    for p in range(3):
        a1, a2, a3 = PARTS[p][2]
        local[p].wait()
        for d in (1, 2, 3):
            first[p, d].wait_recv()
        rest = "".join(a for a in "xyz" if a != a1)

        @pl.loop(0, 16)
        def _(k):
            i = loop_index(rest, k)
            total = own[p][i].astype(jnp.float32)
            for d in range(3):
                total += ra[p][(d,) + i].astype(jnp.float32)
            sa[p][i] = total

        for d in (2, 1, 3):
            target = shifted(at, a2, d)
            second[p, d] = remote(
                sa[p].at[pick(rest, {a2: target[a2]})], rb[p].at[d - 1], p * 9 + 3 + d - 1, target
            )
    for p in range(3):
        a1, a2, a3 = PARTS[p][2]
        rest = "".join(a for a in "xyz" if a != a1)
        for d in (1, 2, 3):
            second[p, d].wait_recv()

        @pl.loop(0, 4)
        def _(k):
            i = loop_index(a3, k)
            coordinate = i[0] if len(i) == 1 else i[1] * 2 + i[0]
            total = sa[p][pick(rest, {a2: at[a2], a3: coordinate})]
            for d in range(3):
                total += rb[p][(d,) + i]
            sb[p][i] = total

        for d in (2, 1, 3):
            target = shifted(at, a3, d)
            third[p, d] = remote(
                sb[p].at[pick(a3, {a3: target[a3]})], rc[p].at[d - 1], p * 9 + 6 + d - 1, target
            )
    wcopy.wait()

    @pl.loop(0, RB)
    def _(j):
        here = pl.ds(j * TILE, TILE)
        wout[here, :] = home[here, :] + rw[here, :].astype(jnp.float32)

    for p in range(3):
        a1, a2, a3 = PARTS[p][2]
        for d in (1, 2, 3):
            third[p, d].wait_recv()
        total = sb[p][pick(a3, {a3: at[a3]})]
        for d in range(3):
            total += rc[p][d]
        jout[rows(p), :] = total
    for c in list(first.values()) + list(second.values()) + list(third.values()):
        c.wait_send()


def scatter(jobs, away, home):
    hbm = pl.BlockSpec(memory_space=pl.ANY)
    vmem = pl.BlockSpec(memory_space=pltpu.VMEM)
    own, ra, sa, rb, sb, rc = [], [], [], [], [], []
    for _, n, (a1, a2, a3) in PARTS:
        after = dims_of("".join(a for a in "xyz" if a != a1)) + (n, TILE)
        last = dims_of(a3) + (n, TILE)
        own.append(pltpu.VMEM(after, jnp.bfloat16))
        ra.append(pltpu.VMEM((3,) + after, jnp.bfloat16))
        sa.append(pltpu.VMEM(after, jnp.float32))
        rb.append(pltpu.VMEM((3,) + last, jnp.float32))
        sb.append(pltpu.VMEM(last, jnp.float32))
        rc.append(pltpu.VMEM((3, n, TILE), jnp.float32))
    return pl.pallas_call(
        scatter_kernel,
        in_specs=[hbm, hbm, vmem],
        out_specs=[vmem, vmem],
        out_shape=[
            jax.ShapeDtypeStruct((JLOC, TILE), jnp.float32),
            jax.ShapeDtypeStruct((NW_LOC, TILE), jnp.float32),
        ],
        scratch_shapes=own
        + ra
        + sa
        + rb
        + sb
        + rc
        + [
            pltpu.VMEM((NW_LOC, TILE), jnp.bfloat16),
            pltpu.SemaphoreType.DMA((3,)),
            pltpu.SemaphoreType.DMA,
            pltpu.SemaphoreType.DMA,
            pltpu.SemaphoreType.DMA((27,)),
            pltpu.SemaphoreType.DMA((27,)),
        ],
        compiler_params=pltpu.CompilerParams(
            collective_id=1, has_side_effects=True, vmem_limit_bytes=56 * 2**20
        ),
        name="scatter_sums",
    )(jobs, away, home)


def on_device(
    worker_emb,
    job_emb,
    worker_cot,
    job_cot,
    worker_deg,
    job_deg,
    block_rows,
    block_cols,
    block_tiles,
    live_count,
):
    quarter = worker_emb.shape[1]
    worker_scale = lax.rsqrt(worker_deg.astype(jnp.float32))[:, None]
    job_scale = lax.rsqrt(job_deg.astype(jnp.float32))[:, None]
    worker_src = jnp.concatenate(
        [worker_emb * worker_scale, worker_cot * worker_scale], axis=1
    ).astype(jnp.bfloat16)
    job_src = jnp.concatenate([job_emb * job_scale, job_cot * job_scale], axis=1).astype(
        jnp.bfloat16
    )
    live = jnp.broadcast_to(live_count[0, 0], (NB,))
    x_lo = jnp.broadcast_to((lax.axis_index("col") // 2).astype(jnp.int32), (NB,))
    zero = jnp.zeros((NB,), jnp.int32)
    meta = jnp.stack([block_rows, block_cols, live, x_lo, zero, zero, zero, zero])
    table, workers, tiles, metas = gather(worker_src, job_src, block_tiles, meta)
    jobs, away, home = sparse_products(
        metas,
        table.reshape(2, NJ, TILE),
        workers,
        tiles.reshape(2 * NB, TILE, TILE),
    )
    job_part, worker_part = scatter(jobs.reshape(dims_of("xyz") + (JLOC, TILE)), away, home)
    worker_out = worker_scale * worker_part[:, :quarter]
    worker_grad = worker_scale * worker_part[:, quarter:]
    job_out = job_scale * job_part[:, :quarter]
    job_grad = job_scale * job_part[:, quarter:]
    return (worker_out, job_out, worker_grad, job_grad)


def solution(mesh):
    return jax.shard_map(
        on_device,
        mesh=mesh,
        in_specs=(
            P("blk", "col"),
            P("blk", "col"),
            P("blk", "col"),
            P("blk", "col"),
            P("blk"),
            P("blk"),
            P(("blk", "col")),
            P(("blk", "col")),
            P(("blk", "col"), None, None),
            P("blk", "col"),
        ),
        out_specs=(P("blk", "col"), P("blk", "col"), P("blk", "col"), P("blk", "col")),
        check_vma=False,
    )
```

time: 705 us -> 121 us (0.17)
  waiting for transfers between devices: 419 us -> 0 us
  other arithmetic: 153 us -> 6.98 us
  Pallas kernels: 0 us -> 102 us
  local copies, waits for them, and re-layouts: 68.4 us -> 9.55 us
  matrix products: 40.3 us -> 0 us
  between operations: 14.5 us -> 1.39 us
    reduce_scatter x3 -> x0, waiting for transfers between devices: 288 us -> none  [the longest x1 226 us: on_device(): lax.psum_scatter(job_partial, 'blk', scatter_dimension=0, tiled=True)]
    scatter-add x2 -> x0, other arithmetic: 146 us -> none  [the longest x1 73.2 us: on_device(): jax.ops.segment_sum(flipped, block_cols, num_segments=job_block_count)]
    all_gather x2 -> x0, waiting for transfers between devices: 131 us -> none  [the longest x1 101 us: on_device(): job_table = lax.all_gather(job_full, 'blk', axis=0, tiled=True)]
    pallas_call x0 -> x3, Pallas kernels: none -> 102 us  [the longest x1 51.5 us: scatter(): pl.pallas_call(scatter_kernel, in_specs=[hbm, hbm, vmem], out_specs=[vmem...]
    dot_general x2 -> x0, matrix products: 40.3 us -> none  [the longest x1 20.2 us: on_device(): jnp.einsum('sji,sjk->sik', dense, worker_blocks, preferred_element_type=j...]
    reshape x2 -> x0, local copies, waits for them, and re-layouts: 22.9 us -> none  [the longest x1 17.4 us: on_device(): jax.ops.segment_sum(flipped, block_cols, num_segments=job_block_count)]
    gather x2 -> x0, local copies, waits for them, and re-layouts: 20.2 us -> none  [the longest x1 11.8 us: on_device(): job_blocks = job_table.reshape(-1, tile_size, width)[block_cols]]
    all_gather x2 -> x0, local copies, waits for them, and re-layouts: 14.7 us -> none  [the longest x1 11.9 us: on_device(): job_table = lax.all_gather(job_full, 'blk', axis=0, tiled=True)]
  transfers between devices with their start and end apart: 5 -> 0, of which waited for: 5 -> 0; matrix products, arithmetic and copies ran while one was open for 0% -> 0% of each run, Pallas kernels for 0% -> 0%
where the time goes in v1:
time: 121 us; the launch traced here: 120 us
  Pallas kernels  102 us (84%)
  local copies, waits for them, and re-layouts  9.55 us (8%)
  other arithmetic  6.98 us (6%)
  between operations  1.39 us (1%)
    pallas_call x1, Pallas kernels, scatter(): pl.pallas_call(scatter_kernel, in_specs=[hbm, hbm, vmem], out_specs=[vmem...  51.5 us
    pallas_call x1, Pallas kernels, gather(): pl.pallas_call(gather_kernel, in_specs=[hbm] * 4, out_specs=[hbm] * 4, ou...  39.2 us
    pallas_call x1, Pallas kernels, sparse_products(): pl.pallas_call(sparse_kernel, grid_spec=pltpu.PrefetchScalarGridSpec(num_...  11.7 us
    unnamed x8, local copies, waits for them, and re-layouts  8.26 us

profile of v1, /device:TPU:0, one launch (start us, length us, event | category | flops | bytes accessed | tf_op | source)
XLA Modules:
  0.0 120.4 jit_solution(6023546875578590159)
XLA Ops:
  1.3 0.7 convert_rsqrt_fusion.1
  2.0 1.3 %stack.15.meta = s32[8,128]{1,0:T(8,128)} concatenate(s32[1,128]{1,0:T(1,128)} %bitcast.8, s32[1,128]{1,0:T(1,128)} %bitcast.9, s32[1,128]{1,0:T(1,128)S(1)} %stack_broadcast_in_dim.6, s32[1,128]{1,0:T(1,128)S(1)} %stack_broadcast_in_dim.7, s32[4,128]{1,0:T(4,128)S(1)} %stack.14), dimensions={0} | concatenate | bytes 8192 | tf_op jit(solution)/shard_map/stack | solution.py:573
  3.3 0.7 convert_rsqrt_fusion
  4.0 0.9 copy.16
  4.9 0.9 copy.17
  5.9 0.1 multiply_convert_fusion.3
  6.0 0.7 pad_maximum_fusion.1.jsrc
  6.7 1.4 %copy.14 = f32[2048,64]{1,0:T(8,128)S(1)} copy(f32[2048,64]{0,1:T(8,128)} %param.10) | data formatting | bytes 1048576 | tf_op args[0]
  8.1 1.4 %copy.15 = f32[2048,64]{1,0:T(8,128)S(1)} copy(f32[2048,64]{0,1:T(8,128)} %param.12) | data formatting | bytes 1048576 | tf_op args[2]
  9.4 0.3 multiply_convert_fusion.1
  9.8 1.1 pad_maximum_fusion.wsrc
  10.9 39.2 %gather_all.1 = (bf16[2,4,2,4,256,128]{5,4,3,2,1,0:T(8,128)(2,1)}, bf16[2,2048,128]{2,1,0:T(8,128)(2,1)}, bf16[2,128,128,128]{3,2,1,0:T(8,128)(2,1)}, s32[2,8,128]{2,1,0:T(8,128)}) custom-call(bf16[2048,128]{1,0:T(8,128)(2,1)} %pad_maximum_fusion.wsrc, bf16[256,128]{1,0:T(8,128)(2,1)} %pad_maximum_fusion.1.jsrc, s32[128,128,128]{2,1,0:T(8,128)} %tiles.1, ...), custom_call_target="tpu_custom_call" | custom-call | tf_op jit(solution)/shard_map/gather_all/pallas_call | solution.py:208
  50.1 11.7 %sparse_products.1 = (bf16[2,8192,128]{2,1,0:T(8,128)(2,1)}, bf16[2048,128]{1,0:T(8,128)(2,1)}, f32[2048,128]{1,0:T(8,128)}) custom-call(s32[2,8,128]{2,1,0:T(8,128)} %get-tuple-element.13.meta, bf16[2,8192,128]{2,1,0:T(8,128)(2,1)} %bitcast.11, bf16[2,2048,128]{2,1,0:T(8,128)(2,1)} %get-tuple-element.15.workers, bf16[256,128,128]{2,1,0:T(8,128)(2,1)} %bitcast.10), custom_call_target="tpu_custom_call" | custom-call | flops 4294967296 | bytes 23068672 | tf_op jit(solution)/shard_map/sparse_products/pallas_call | solution.py:328
  61.9 51.5 %scatter_sums.1 = (f32[256,128]{1,0:T(8,128)}, f32[2048,128]{1,0:T(8,128)}) custom-call(bf16[2,4,2,4,256,128]{5,4,3,2,1,0:T(8,128)(2,1)} %bitcast.7, bf16[2048,128]{1,0:T(8,128)(2,1)} %get-tuple-element.18.away, f32[2048,128]{1,0:T(8,128)} %get-tuple-element.19.home), custom_call_target="tpu_custom_call" | custom-call | tf_op jit(solution)/shard_map/scatter_sums/pallas_call | solution.py:520
  113.3 1.1 slice_multiply_fusion.2
  114.5 0.7 copy.21
  115.2 0.7 copy.19
  115.9 2.2 %slice_multiply_fusion = (f32[2048,64]{1,0:T(8,128)S(1)}, f32[2048,64]{1,0:T(8,128)S(1)}) fusion(f32[2048,128]{1,0:T(8,128)} %get-tuple-element.20, f32[2048]{0:T(1024)S(1)} %convert_rsqrt_fusion), kind=kLoop, calls=%fused_computation | loop fusion | flops 262144 | bytes 2105344 | tf_op jit(solution)/shard_map/mul | solution.py:583
  118.1 1.1 copy.20
  119.2 1.1 copy.18
  (3 shorter events, 0.0 us)

commit v2 on v0

v2 whole, which is shorter than its diff:
```python
import jax
import jax.numpy as jnp
from jax import lax
from jax.experimental import pallas as pl
from jax.experimental.pallas import tpu as pltpu
from jax.sharding import PartitionSpec as P

MESH = pl.DeviceIdType.MESH
TILE = 128
NB = 128
RB = 16
NJB = 64
NW_LOC = RB * TILE
NJ = NJB * TILE
JLOC = 256
PARTS = ((0, 32, "xyz"), (32, 48, "yzx"), (80, 48, "zxy"))
DIMS = (("x", 2), ("z", 4), ("x", 2), ("y", 4))
TCHUNK = 8
NCHUNK = NB // TCHUNK
NBUF = 4
GROUP = 16
SLOTS = 2 * NB


def position():
    blk = lax.axis_index("blk")
    col = lax.axis_index("col")
    return {
        "z": blk // 8,
        "x": ((blk // 4) % 2) * 2 + col // 2,
        "y": blk % 4,
        "core": col % 2,
    }


def device(at):
    x = at["x"]
    return (at["z"] * 8 + (x // 2) * 4 + at["y"], (x % 2) * 2 + at["core"])


def shifted(at, axis, by):
    return {**at, axis: (at[axis] + by + 4) % 4}


def neighbours(at):
    out = [device(shifted(at, axis, d)) for axis in "xyz" for d in (1, 2, 3)]
    out.append(device({**at, "core": 1 - at["core"]}))
    return out


def dims_of(axes):
    return tuple(n for name, n in DIMS if name in axes)


def pick(axes, fixed):
    index = []
    seen_x = False
    for name, _ in DIMS:
        if name not in axes:
            continue
        if name not in fixed:
            index.append(slice(None))
        elif name == "x":
            index.append(fixed["x"] // 2 if seen_x else fixed["x"] % 2)
        else:
            index.append(fixed[name])
        if name == "x":
            seen_x = True
    return tuple(index)


def part_rows(p):
    return pl.ds(PARTS[p][0], PARTS[p][1])


def chunk_part(ref, p, fixed):
    return ref.at[pick("xyz", fixed) + (slice(None), part_rows(p), slice(None))]


def loop_index(axes, k):
    index = []
    for n in reversed(dims_of(axes)):
        index.append(k % n)
        k = k // n
    return tuple(reversed(index))


def block_index(j):
    return (j >> 4, (j >> 3) & 1, (j >> 1) & 3, j & 1)


def order_slots(meta, table):
    lane = lax.broadcasted_iota(jnp.int32, (1, NB), 1)
    place = lax.broadcasted_iota(jnp.int32, (NB, SLOTS), 1)
    block = lax.broadcasted_iota(jnp.int32, (NB, NB), 1)

    def column(row):
        return jnp.transpose(jnp.broadcast_to(row, (NB, NB)))

    def count_down(flags):
        return jnp.sum(jnp.where(flags, 1, 0), axis=0, keepdims=True)

    payloads, cols, rows = [], [], []
    for h in range(2):
        ok = lane < meta[h, 2:3, :]
        r, c = meta[h, 0:1, :], meta[h, 1:2, :]
        payloads.append(lane + h * NB + r * SLOTS + c * (SLOTS * RB))
        cols.append(jnp.where(ok, c, NJB))
        rows.append(jnp.where(ok, r, RB))
    for line, (keys, at) in enumerate(((cols, 2), (rows, 4))):
        unique = [keys[h] * SLOTS + lane + h * NB for h in range(2)]
        across = jnp.broadcast_to(jnp.concatenate(unique, axis=1), (NB, SLOTS))
        rank = jnp.zeros((1, SLOTS), jnp.int32)
        for h in range(2):
            down = column(unique[h])
            rank += count_down(jnp.concatenate([down, down], axis=1) < across)
        ordered = jnp.zeros((1, SLOTS), jnp.int32)
        upto = jnp.zeros((1, NB), jnp.int32)
        count = jnp.zeros((1, NB), jnp.int32)
        for h in range(2):
            spot = column(rank[:, h * NB : (h + 1) * NB])
            hit = place == jnp.concatenate([spot, spot], axis=1)
            value = column(payloads[h])
            value = jnp.concatenate([value, value], axis=1)
            ordered += jnp.sum(jnp.where(hit, value, 0), axis=0, keepdims=True)
            key = column(keys[h])
            upto += count_down(key <= block)
            count += count_down(key == block)
        table[line : line + 1, :] = ordered
        table[at : at + 1, :NB] = jnp.maximum(upto - 1, 0)
        table[at + 1 : at + 2, :NB] = count


def layer_kernel(
    wemb,
    wcot,
    jemb,
    jcot,
    wdeg,
    jdeg,
    brows,
    bcols,
    live,
    tiles,
    wsum,
    jsum,
    wbuf,
    dense_in,
    tin,
    xbuf,
    table,
    rows_in,
    meta,
    order,
    slots,
    cbuf,
    jobs,
    away,
    home,
    rw,
    ra0,
    ra1,
    ra2,
    sa0,
    sa1,
    sa2,
    rb0,
    rb1,
    rb2,
    sb0,
    sb1,
    sb2,
    rc0,
    rc1,
    rc2,
    in_sem,
    tin_sem,
    tsend,
    trecv,
    osend,
    orecv,
    gsend,
    grecv,
    ssend,
    srecv,
):
    ra, sa = (ra0, ra1, ra2), (sa0, sa1, sa2)
    rb, sb, rc = (rb0, rb1, rb2), (sb0, sb1, sb2), (rc0, rc1, rc2)
    at = position()
    x_lo = at["x"] % 2
    core = at["core"]
    core_mate = {**at, "core": 1 - core}
    x_mate = {**at, "x": at["x"] + 1 - 2 * x_lo}
    f32, bf16 = jnp.float32, jnp.bfloat16

    def load(i):
        return pltpu.make_async_copy(
            tiles.at[pl.ds(i * TCHUNK, TCHUNK)], tin.at[i % NBUF], tin_sem.at[i % NBUF]
        )

    def remote(src, dst, sems, rems, i, target):
        c = pltpu.make_async_remote_copy(
            src_ref=src,
            dst_ref=dst,
            send_sem=sems.at[i],
            recv_sem=rems.at[i],
            device_id=device(target),
            device_id_type=MESH,
        )
        c.start()
        return c

    barrier = pltpu.get_barrier_semaphore()
    others = neighbours(at)
    for other in others:
        pl.semaphore_signal(barrier, inc=1, device_id=other, device_id_type=MESH)
    ins = [
        pltpu.make_async_copy(jemb, rows_in.at[pl.ds(0, 64)], in_sem.at[0]),
        pltpu.make_async_copy(jcot, rows_in.at[pl.ds(64, 64)], in_sem.at[1]),
        pltpu.make_async_copy(wemb, dense_in.at[pl.ds(0, 64)], in_sem.at[2]),
        pltpu.make_async_copy(wcot, dense_in.at[pl.ds(64, 64)], in_sem.at[3]),
    ]
    for c in ins:
        c.start()
    for i in range(NBUF):
        load(i).start()

    job_scale = lax.rsqrt(jdeg[...].astype(f32))
    worker_scale = lax.rsqrt(wdeg[...].astype(f32))
    meta[core] = jnp.zeros((8, NB), jnp.int32)
    order[...] = jnp.zeros((8, SLOTS), jnp.int32)
    meta[core, 0:1, :] = brows[...]
    meta[core, 1:2, :] = bcols[...]
    meta[core, 2:3, :] = jnp.broadcast_to(live[...], (1, NB))
    ins[0].wait()
    ins[1].wait()
    for i in range(2):
        here = slice(i * TILE, (i + 1) * TILE)
        table[pick("xyz", at) + (i,)] = jnp.transpose(
            rows_in[:, here] * job_scale[:, here]
        ).astype(bf16)
    pl.semaphore_wait(barrier, len(others))
    first, second, third = {}, {}, {}
    for d in (1, 3, 2):
        for p in range(3):
            own = chunk_part(table, p, at)
            first[p, d] = remote(
                own, own, gsend, grecv, p * 18 + d - 1, shifted(at, PARTS[p][2][0], d)
            )
    mcopy = remote(meta.at[core], meta.at[core], osend, orecv, 0, core_mate)
    ins[2].wait()
    ins[3].wait()
    for i in range(RB):
        here = slice(i * TILE, (i + 1) * TILE)
        wbuf[x_lo, i] = jnp.transpose(dense_in[:, here] * worker_scale[:, here]).astype(bf16)
    wcopy = remote(wbuf.at[x_lo], wbuf.at[x_lo], osend, orecv, 1, x_mate)

    tcopies = []

    def chunk(i):
        load(i).wait()
        here = pl.ds(core * NB + i * TCHUNK, TCHUNK)
        xbuf[here] = tin[i % NBUF].astype(f32).astype(bf16)
        if i + NBUF < NCHUNK:
            load(i + NBUF).start()
        tcopies.append(remote(xbuf.at[here], xbuf.at[here], tsend, trecv, i, core_mate))

    for i in range(NCHUNK // 2):
        chunk(i)
    for p in range(3):
        a1, a2, a3 = PARTS[p][2]
        for d in (1, 2, 3):
            first[p, d].wait_recv()
        own = chunk_part(table, p, {a2: at[a2], a3: at[a3]})
        for d in (1, 3, 2):
            second[p, d] = remote(own, own, gsend, grecv, p * 18 + 3 + d - 1, shifted(at, a2, d))
    for p in range(3):
        a1, a2, a3 = PARTS[p][2]
        own = chunk_part(table, p, {a2: at[a2], a3: at[a3]})
        for d in (1, 3, 2):
            third[p, 0, d] = remote(own, own, gsend, grecv, p * 18 + 6 + d - 1, shifted(at, a3, d))
    for i in range(NCHUNK // 2, NCHUNK):
        chunk(i)
    for g in (1, 3, 2):
        for p in range(3):
            a1, a2, a3 = PARTS[p][2]
            second[p, g].wait_recv()
            got = chunk_part(table, p, {a2: (at[a2] - g + 4) % 4, a3: at[a3]})
            for d in (1, 3, 2):
                third[p, g, d] = remote(
                    got, got, gsend, grecv, p * 18 + 6 + g * 3 + d - 1, shifted(at, a3, d)
                )
    mcopy.wait()
    order_slots(meta, order)
    to_scalars = pltpu.make_async_copy(order, slots, in_sem.at[0])
    to_scalars.start()
    to_scalars.wait()
    for c in tcopies:
        c.wait_recv()
    wcopy.wait()

    def running(line, product, key):
        def step(q, total):
            for g in range(GROUP):
                k = q * GROUP + g
                entry = slots[line, k]
                before = slots[line, jnp.maximum(k - 1, 0)]
                fresh = key(entry) != key(before)
                total = jnp.where(fresh, 0.0, total) + product(
                    entry & (SLOTS - 1), (entry >> 8) & (RB - 1), (entry >> 12) & (NJB - 1)
                )
                cbuf[k, 0] = total[:, :TILE].astype(bf16)
                cbuf[k, 1] = total[:, TILE:].astype(bf16)
            return total

        lax.fori_loop(0, SLOTS // GROUP, step, jnp.zeros((TILE, 2 * TILE), f32))

    def to_jobs(s, r, c):
        workers = jnp.concatenate([wbuf[0, r], wbuf[1, r]], axis=1)
        return lax.dot_general(
            xbuf[s], workers, (((0,), (0,)), ((), ())), preferred_element_type=f32
        )

    def to_workers(s, r, c):
        i = block_index(c)
        rows = jnp.concatenate([table[(0,) + i], table[(1,) + i]], axis=1)
        return jnp.dot(xbuf[s], rows, preferred_element_type=f32)

    running(0, to_jobs, lambda entry: entry >> 12)

    @pl.loop(0, NJB)
    def _(j):
        last = slots[2, j] & (SLOTS - 1)
        some = slots[3, j] > 0
        for half in range(2):
            value = cbuf[last, half]
            jobs[(half,) + block_index(j)] = jnp.where(some, value, jnp.zeros_like(value))

    sfirst, ssecond, sthird = {}, {}, {}
    for d in (2, 1, 3):
        for p in range(3):
            a1 = PARTS[p][2][0]
            target = shifted(at, a1, d)
            sfirst[p, d] = remote(
                chunk_part(jobs, p, {a1: target[a1]}),
                ra[p].at[d - 1],
                ssend,
                srecv,
                p * 9 + d - 1,
                target,
            )
    for c in third.values():
        c.wait_recv()
    running(1, to_workers, lambda entry: (entry >> 8) & (RB - 1))

    @pl.loop(0, RB)
    def _(j):
        last = slots[4, j] & (SLOTS - 1)
        some = slots[5, j] > 0
        for ref, half in ((away, 1 - x_lo), (home, x_lo)):
            value = cbuf[last, half]
            ref[j] = jnp.where(some, value, jnp.zeros_like(value))

    acopy = remote(away, rw, osend, orecv, 2, x_mate)

    for p in range(3):
        a1, a2, a3 = PARTS[p][2]
        for d in (1, 2, 3):
            sfirst[p, d].wait_recv()
        rest = "".join(a for a in "xyz" if a != a1)
        rows = part_rows(p)

        @pl.loop(0, 16)
        def _(k):
            i = loop_index(rest, k)
            others = iter(i)
            mine = iter((at["x"] % 2, at["x"] // 2) if a1 == "x" else (at[a1],))
            here = tuple(next(mine) if name == a1 else next(others) for name, _ in DIMS)
            total = jobs[here + (slice(None), rows, slice(None))].astype(f32)
            for d in range(3):
                total += ra[p][(d,) + i].astype(f32)
            sa[p][i] = total

        for d in (2, 1, 3):
            target = shifted(at, a2, d)
            ssecond[p, d] = remote(
                sa[p].at[pick(rest, {a2: target[a2]})],
                rb[p].at[d - 1],
                ssend,
                srecv,
                p * 9 + 3 + d - 1,
                target,
            )
    for p in range(3):
        a1, a2, a3 = PARTS[p][2]
        rest = "".join(a for a in "xyz" if a != a1)
        for d in (1, 2, 3):
            ssecond[p, d].wait_recv()

        @pl.loop(0, 4)
        def _(k):
            i = loop_index(a3, k)
            coordinate = i[0] if len(i) == 1 else i[1] * 2 + i[0]
            total = sa[p][pick(rest, {a2: at[a2], a3: coordinate})]
            for d in range(3):
                total += rb[p][(d,) + i]
            sb[p][i] = total

        for d in (2, 1, 3):
            target = shifted(at, a3, d)
            sthird[p, d] = remote(
                sb[p].at[pick(a3, {a3: target[a3]})],
                rc[p].at[d - 1],
                ssend,
                srecv,
                p * 9 + 6 + d - 1,
                target,
            )
    acopy.wait()
    for i in range(RB):
        here = slice(i * TILE, (i + 1) * TILE)
        wsum[here, :] = home[i].astype(f32) + rw[i].astype(f32)
    for p in range(3):
        a1, a2, a3 = PARTS[p][2]
        for d in (1, 2, 3):
            sthird[p, d].wait_recv()
        total = sb[p][pick(a3, {a3: at[a3]})]
        for d in range(3):
            total += rc[p][d]
        jsum[:, part_rows(p), :] = total
    for copies in (first, second, third, sfirst, ssecond, sthird):
        for c in copies.values():
            c.wait_send()
    for c in tcopies:
        c.wait_send()


def layer(wemb, wcot, jemb, jcot, wdeg, jdeg, brows, bcols, live, tiles):
    hbm = pl.BlockSpec(memory_space=pl.ANY)
    vmem = pl.BlockSpec(memory_space=pltpu.VMEM)
    ra, sa, rb, sb, rc = [], [], [], [], []
    for _, n, (a1, a2, a3) in PARTS:
        after = dims_of("".join(a for a in "xyz" if a != a1)) + (2, n, TILE)
        last = dims_of(a3) + (2, n, TILE)
        ra.append(pltpu.VMEM((3,) + after, jnp.bfloat16))
        sa.append(pltpu.VMEM(after, jnp.float32))
        rb.append(pltpu.VMEM((3,) + last, jnp.float32))
        sb.append(pltpu.VMEM(last, jnp.float32))
        rc.append(pltpu.VMEM((3, 2, n, TILE), jnp.float32))
    chunks = dims_of("xyz") + (2, TILE, TILE)
    dma = pltpu.SemaphoreType.DMA
    return pl.pallas_call(
        layer_kernel,
        in_specs=[hbm] * 4 + [vmem] * 5 + [hbm],
        out_specs=[vmem] * 2,
        out_shape=[
            jax.ShapeDtypeStruct((NW_LOC, TILE), jnp.float32),
            jax.ShapeDtypeStruct((2, TILE, TILE), jnp.float32),
        ],
        scratch_shapes=[
            pltpu.VMEM((2, RB, TILE, TILE), jnp.bfloat16),
            pltpu.VMEM((TILE, NW_LOC), jnp.float32),
            pltpu.VMEM((NBUF, TCHUNK, TILE, TILE), jnp.int32),
            pltpu.VMEM((SLOTS, TILE, TILE), jnp.bfloat16),
            pltpu.VMEM(chunks, jnp.bfloat16),
            pltpu.VMEM((TILE, JLOC), jnp.float32),
            pltpu.VMEM((2, 8, NB), jnp.int32),
            pltpu.VMEM((8, SLOTS), jnp.int32),
            pltpu.SMEM((8, SLOTS), jnp.int32),
            pltpu.VMEM((SLOTS, 2, TILE, TILE), jnp.bfloat16),
            pltpu.VMEM(chunks, jnp.bfloat16),
            pltpu.VMEM((RB, TILE, TILE), jnp.bfloat16),
            pltpu.VMEM((RB, TILE, TILE), jnp.bfloat16),
            pltpu.VMEM((RB, TILE, TILE), jnp.bfloat16),
        ]
        + ra
        + sa
        + rb
        + sb
        + rc
        + [
            dma((4,)),
            dma((NBUF,)),
            dma((NCHUNK,)),
            dma((NCHUNK,)),
            dma((3,)),
            dma((3,)),
            dma((54,)),
            dma((54,)),
            dma((27,)),
            dma((27,)),
        ],
        compiler_params=pltpu.CompilerParams(
            collective_id=0, has_side_effects=True, vmem_limit_bytes=60 * 2**20
        ),
        name="layer",
    )(wemb, wcot, jemb, jcot, wdeg, jdeg, brows, bcols, live, tiles)


def finish_kernel(wsum, jsum, wdeg, jdeg, wout, wgrad, jout, jgrad):
    for total, deg, out, grad in ((wsum, wdeg, wout, wgrad), (jsum, jdeg, jout, jgrad)):
        scale = lax.rsqrt(deg[...].astype(jnp.float32))
        for i in range(total.shape[0] // TILE):
            here = slice(i * TILE, (i + 1) * TILE)
            value = jnp.transpose(total[here, :]) * scale[:, here]
            out[:, here] = value[:64]
            grad[:, here] = value[64:]


def finish(wsum, jsum, wdeg, jdeg):
    vmem = pl.BlockSpec(memory_space=pltpu.VMEM)
    return pl.pallas_call(
        finish_kernel,
        in_specs=[vmem] * 4,
        out_specs=[vmem] * 4,
        out_shape=[
            jax.ShapeDtypeStruct((64, NW_LOC), jnp.float32),
            jax.ShapeDtypeStruct((64, NW_LOC), jnp.float32),
            jax.ShapeDtypeStruct((64, JLOC), jnp.float32),
            jax.ShapeDtypeStruct((64, JLOC), jnp.float32),
        ],
        name="finish",
    )(wsum, jsum, wdeg, jdeg)


def on_device(
    worker_emb,
    job_emb,
    worker_cot,
    job_cot,
    worker_deg,
    job_deg,
    block_rows,
    block_cols,
    block_tiles,
    live_count,
):
    wdeg, jdeg = worker_deg[None, :], job_deg[None, :]
    wsum, jsum = layer(
        worker_emb.T,
        worker_cot.T,
        job_emb.T,
        job_cot.T,
        wdeg,
        jdeg,
        block_rows[None, :],
        block_cols[None, :],
        live_count,
        block_tiles,
    )
    worker_out, worker_grad, job_out, job_grad = finish(wsum, jsum.reshape(JLOC, TILE), wdeg, jdeg)
    return (worker_out.T, job_out.T, worker_grad.T, job_grad.T)


def solution(mesh):
    return jax.shard_map(
        on_device,
        mesh=mesh,
        in_specs=(
            P("blk", "col"),
            P("blk", "col"),
            P("blk", "col"),
            P("blk", "col"),
            P("blk"),
            P("blk"),
            P(("blk", "col")),
            P(("blk", "col")),
            P(("blk", "col"), None, None),
            P("blk", "col"),
        ),
        out_specs=(P("blk", "col"), P("blk", "col"), P("blk", "col"), P("blk", "col")),
        check_vma=False,
    )
```

time: 705 us -> 84.6 us (0.12)
  waiting for transfers between devices: 419 us -> 0 us
  other arithmetic: 153 us -> 0 us
  Pallas kernels: 0 us -> 83.1 us
  local copies, waits for them, and re-layouts: 68.4 us -> 0 us
  matrix products: 40.3 us -> 0 us
  between operations: 14.5 us -> 1.29 us
    reduce_scatter x3 -> x0, waiting for transfers between devices: 288 us -> none  [the longest x1 226 us: on_device(): lax.psum_scatter(job_partial, 'blk', scatter_dimension=0, tiled=True)]
    scatter-add x2 -> x0, other arithmetic: 146 us -> none  [the longest x1 73.2 us: on_device(): jax.ops.segment_sum(flipped, block_cols, num_segments=job_block_count)]
    all_gather x2 -> x0, waiting for transfers between devices: 131 us -> none  [the longest x1 101 us: on_device(): job_table = lax.all_gather(job_full, 'blk', axis=0, tiled=True)]
    pallas_call x0 -> x2, Pallas kernels: none -> 83.1 us  [the longest x1 80.5 us: layer(): pl.pallas_call(layer_kernel, in_specs=[hbm] * 4 + [vmem] * 5 + [hbm], out...]
    dot_general x2 -> x0, matrix products: 40.3 us -> none  [the longest x1 20.2 us: on_device(): jnp.einsum('sji,sjk->sik', dense, worker_blocks, preferred_element_type=j...]
    reshape x2 -> x0, local copies, waits for them, and re-layouts: 22.9 us -> none  [the longest x1 17.4 us: on_device(): jax.ops.segment_sum(flipped, block_cols, num_segments=job_block_count)]
    gather x2 -> x0, local copies, waits for them, and re-layouts: 20.2 us -> none  [the longest x1 11.8 us: on_device(): job_blocks = job_table.reshape(-1, tile_size, width)[block_cols]]
    all_gather x2 -> x0, local copies, waits for them, and re-layouts: 14.7 us -> none  [the longest x1 11.9 us: on_device(): job_table = lax.all_gather(job_full, 'blk', axis=0, tiled=True)]
  transfers between devices with their start and end apart: 5 -> 0, of which waited for: 5 -> 0; matrix products, arithmetic and copies ran while one was open for 0% -> 0% of each run, Pallas kernels for 0% -> 0%
where the time goes in v2:
time: 84.6 us; the launch traced here: 84.4 us
  Pallas kernels  83.1 us (98%)
  between operations  1.29 us (2%)
    pallas_call x1, Pallas kernels, layer(): pl.pallas_call(layer_kernel, in_specs=[hbm] * 4 + [vmem] * 5 + [hbm], out...  80.5 us
    pallas_call x1, Pallas kernels, finish(): pl.pallas_call(finish_kernel, in_specs=[vmem] * 4, out_specs=[vmem] * 4,...  2.63 us

profile of v2, /device:TPU:0, one launch (start us, length us, event | category | flops | bytes accessed | tf_op | source)
XLA Modules:
  0.0 84.4 jit_solution(5355718597532001905)
XLA Ops:
  1.3 80.5 %layer.1 = (f32[2048,128]{1,0:T(8,128)}, f32[2,128,128]{2,1,0:T(8,128)}) custom-call(f32[64,2048]{1,0:T(8,128)} %bitcast.13, f32[64,2048]{1,0:T(8,128)} %bitcast.14, f32[64,256]{1,0:T(8,128)} %bitcast.16, f32[64,256]{1,0:T(8,128)} %bitcast.17, s32[1,2048]{1,0:T(1,128)} %bitcast.18, s32[1,256]{1,0:T(1,128)} %bitcast.20, s32[1,128]{1,0:T(1,128)} %bitcast.22, ...), custom_call_target="tpu_custom_call" | custom-call | tf_op jit(solution)/shard_map/layer/pallas_call | solution.py:452
  81.8 2.6 %finish.1 = (f32[64,2048]{1,0:T(8,128)}, f32[64,2048]{1,0:T(8,128)}, f32[64,256]{1,0:T(8,128)}, f32[64,256]{1,0:T(8,128)}) custom-call(f32[2048,128]{1,0:T(8,128)} %get-tuple-element.10.wsum, f32[256,128]{1,0:T(8,128)} %bitcast.15, s32[1,2048]{1,0:T(1,128)} %bitcast.19, s32[1,256]{1,0:T(1,128)} %bitcast.21), custom_call_target="tpu_custom_call" | custom-call | tf_op jit(solution)/shard_map/finish/pallas_call | solution.py:512

commit v3 on v2

v3 whole, which is shorter than its diff:
```python
import jax
import jax.numpy as jnp
from jax import lax
from jax.experimental import pallas as pl
from jax.experimental.pallas import tpu as pltpu
from jax.sharding import PartitionSpec as P

MESH = pl.DeviceIdType.MESH
TILE = 128
NB = 128
RB = 16
NJB = 64
NW_LOC = RB * TILE
NJ = NJB * TILE
JLOC = 256
SPREAD = ((0, 48, "xyz"), (48, 48, "xzy"), (96, 32, "yzx"))
REDUCE = (
    (0, 48, "yzx", 0),
    (48, 48, "zyx", 0),
    (0, 48, "yzx", 1),
    (48, 48, "zyx", 1),
    (96, 32, "xyz", None),
)
LABELS = {"x_lo": 2, "z": 4, "x_hi": 2, "y": 4}
DIMS = (("x", 2), ("z", 4), ("x", 2), ("y", 4))
TCHUNK = 8
NCHUNK = NB // TCHUNK
NBUF = 4
GROUP = 16
SLOTS = 2 * NB


def position():
    blk = lax.axis_index("blk")
    col = lax.axis_index("col")
    return {
        "z": blk // 8,
        "x": ((blk // 4) % 2) * 2 + col // 2,
        "y": blk % 4,
        "core": col % 2,
    }


def device(at):
    x = at["x"]
    return (at["z"] * 8 + (x // 2) * 4 + at["y"], (x % 2) * 2 + at["core"])


def shifted(at, axis, by):
    return {**at, axis: (at[axis] + by + 4) % 4}


def neighbours(at):
    out = [device(shifted(at, axis, d)) for axis in "xyz" for d in (1, 2, 3)]
    out.append(device({**at, "core": 1 - at["core"]}))
    return out


def dims_of(axes):
    return tuple(n for name, n in DIMS if name in axes)


def pick(axes, fixed):
    index = []
    seen_x = False
    for name, _ in DIMS:
        if name not in axes:
            continue
        if name not in fixed:
            index.append(slice(None))
        elif name == "x":
            index.append(fixed["x"] // 2 if seen_x else fixed["x"] % 2)
        else:
            index.append(fixed[name])
        if name == "x":
            seen_x = True
    return tuple(index)


def part_rows(part):
    return pl.ds(part[0], part[1])


def chunk_part(ref, part, fixed):
    return ref.at[pick("xyz", fixed) + (slice(None), part_rows(part), slice(None))]


def labels_of(axis, coordinate):
    return {"x_lo": coordinate % 2, "x_hi": coordinate // 2} if axis == "x" else {axis: coordinate}


def plan(part):
    _, _, (a1, a2, _), wave = part
    after = [x for x in LABELS if x not in labels_of(a1, 0) and (wave is None or x != "x_lo")]
    return after, [x for x in after if x not in labels_of(a2, 0)]


def index(labels, fixed):
    return tuple(fixed.get(x, slice(None)) for x in labels)


def loop_labels(labels, k):
    fixed = {}
    for x in reversed(labels):
        fixed[x] = k % LABELS[x]
        k = k // LABELS[x]
    return fixed


def block_index(j):
    return (j >> 4, (j >> 3) & 1, (j >> 1) & 3, j & 1)


def order_slots(meta, table):
    lane = lax.broadcasted_iota(jnp.int32, (1, NB), 1)
    place = lax.broadcasted_iota(jnp.int32, (NB, SLOTS), 1)
    block = lax.broadcasted_iota(jnp.int32, (NB, NB), 1)

    def column(row):
        return jnp.transpose(jnp.broadcast_to(row, (NB, NB)))

    def count_down(flags):
        return jnp.sum(jnp.where(flags, 1, 0), axis=0, keepdims=True)

    payloads, cols, rows = [], [], []
    for h in range(2):
        ok = lane < meta[h, 2:3, :]
        r, c = meta[h, 0:1, :], meta[h, 1:2, :]
        payloads.append(lane + h * NB + r * SLOTS + c * (SLOTS * RB))
        cols.append(jnp.where(ok, c, NJB))
        rows.append(jnp.where(ok, r, RB))
    for line, (keys, at) in enumerate(((cols, 2), (rows, 4))):
        unique = [keys[h] * SLOTS + lane + h * NB for h in range(2)]
        across = jnp.broadcast_to(jnp.concatenate(unique, axis=1), (NB, SLOTS))
        rank = jnp.zeros((1, SLOTS), jnp.int32)
        for h in range(2):
            down = column(unique[h])
            rank += count_down(jnp.concatenate([down, down], axis=1) < across)
        ordered = jnp.zeros((1, SLOTS), jnp.int32)
        upto = jnp.zeros((1, NB), jnp.int32)
        count = jnp.zeros((1, NB), jnp.int32)
        for h in range(2):
            spot = column(rank[:, h * NB : (h + 1) * NB])
            hit = place == jnp.concatenate([spot, spot], axis=1)
            value = column(payloads[h])
            value = jnp.concatenate([value, value], axis=1)
            ordered += jnp.sum(jnp.where(hit, value, 0), axis=0, keepdims=True)
            key = column(keys[h])
            upto += count_down(key <= block)
            count += count_down(key == block)
        table[line : line + 1, :] = ordered
        table[at : at + 1, :NB] = jnp.maximum(upto - 1, 0)
        table[at + 1 : at + 2, :NB] = count


def layer_kernel(
    wemb,
    wcot,
    jemb,
    jcot,
    wdeg,
    jdeg,
    brows,
    bcols,
    live,
    tiles,
    home,
    rw,
    jsum,
    wown,
    wother,
    dense_in,
    tin,
    xbuf,
    table,
    rows_in,
    meta,
    order,
    slots,
    cbuf,
    jobs,
    away,
    kept,
    *rest,
):
    ra, sa, rb, sb, rc = (rest[i : i + len(REDUCE)] for i in range(0, 5 * len(REDUCE), len(REDUCE)))
    in_sem, tin_sem, tsend, trecv, osend, orecv, gsend, grecv, ssend, srecv = rest[5 * len(REDUCE) :]
    at = position()
    x_lo = at["x"] % 2
    core = at["core"]
    core_mate = {**at, "core": 1 - core}
    x_mate = {**at, "x": at["x"] + 1 - 2 * x_lo}
    f32, bf16 = jnp.float32, jnp.bfloat16

    def load(i):
        return pltpu.make_async_copy(
            tiles.at[pl.ds(i * TCHUNK, TCHUNK)], tin.at[i % NBUF], tin_sem.at[i % NBUF]
        )

    def remote(src, dst, sems, rems, i, target):
        c = pltpu.make_async_remote_copy(
            src_ref=src,
            dst_ref=dst,
            send_sem=sems.at[i],
            recv_sem=rems.at[i],
            device_id=device(target),
            device_id_type=MESH,
        )
        c.start()
        return c

    barrier = pltpu.get_barrier_semaphore()
    others = neighbours(at)
    for other in others:
        pl.semaphore_signal(barrier, inc=1, device_id=other, device_id_type=MESH)
    ins = [
        pltpu.make_async_copy(jemb, rows_in.at[pl.ds(0, 64)], in_sem.at[0]),
        pltpu.make_async_copy(jcot, rows_in.at[pl.ds(64, 64)], in_sem.at[1]),
        pltpu.make_async_copy(wemb, dense_in.at[pl.ds(0, 64)], in_sem.at[2]),
        pltpu.make_async_copy(wcot, dense_in.at[pl.ds(64, 64)], in_sem.at[3]),
    ]
    for c in ins:
        c.start()
    for i in range(NBUF):
        load(i).start()

    job_scale = lax.rsqrt(jdeg[...].astype(f32))
    worker_scale = lax.rsqrt(wdeg[...].astype(f32))
    meta[core] = jnp.zeros((8, NB), jnp.int32)
    order[...] = jnp.zeros((8, SLOTS), jnp.int32)
    meta[core, 0:1, :] = brows[...]
    meta[core, 1:2, :] = bcols[...]
    meta[core, 2:3, :] = jnp.broadcast_to(live[...], (1, NB))
    ins[0].wait()
    ins[1].wait()
    for i in range(2):
        here = slice(i * TILE, (i + 1) * TILE)
        table[pick("xyz", at) + (i,)] = jnp.transpose(
            rows_in[:, here] * job_scale[:, here]
        ).astype(bf16)
    pl.semaphore_wait(barrier, len(others))
    first, second, third = {}, {}, {}
    for d in (1, 3, 2):
        for p in range(3):
            own = chunk_part(table, SPREAD[p], at)
            first[p, d] = remote(
                own, own, gsend, grecv, p * 22 + d - 1, shifted(at, SPREAD[p][2][0], d)
            )
    mcopy = remote(meta.at[core], meta.at[core], osend, orecv, 0, core_mate)
    ins[2].wait()
    ins[3].wait()
    for i in range(RB):
        here = slice(i * TILE, (i + 1) * TILE)
        wown[i] = jnp.transpose(dense_in[:, here] * worker_scale[:, here]).astype(bf16)
    wcopy = remote(wown, wother, osend, orecv, 1, x_mate)

    tcopies = []

    def chunk(i):
        load(i).wait()
        here = pl.ds(core * NB + i * TCHUNK, TCHUNK)
        xbuf[here] = tin[i % NBUF].astype(f32).astype(bf16)
        if i + NBUF < NCHUNK:
            load(i + NBUF).start()
        tcopies.append(remote(xbuf.at[here], xbuf.at[here], tsend, trecv, i, core_mate))

    def spread(p, g):
        a1, a2, a3 = SPREAD[p][2]
        got = chunk_part(table, SPREAD[p], {a2: (at[a2] - g + 4) % 4, a3: at[a3]})
        for d in (1, 3, 2):
            third[p, g, d] = remote(
                got, got, gsend, grecv, p * 22 + 6 + g * 4 + d - 1, shifted(at, a3, d)
            )

    for p in range(3):
        a1, a2, a3 = SPREAD[p][2]
        for d in (1, 2, 3):
            first[p, d].wait_recv()
        own = chunk_part(table, SPREAD[p], {a2: at[a2], a3: at[a3]})
        for d in (1, 3, 2):
            second[p, d] = remote(own, own, gsend, grecv, p * 22 + 3 + d - 1, shifted(at, a2, d))
    for p in range(3):
        spread(p, 0)
    for i in range(NCHUNK // 2):
        chunk(i)
    for g in (1, 3, 2):
        for p in range(3):
            second[p, g].wait_recv()
            spread(p, g)
    for i in range(NCHUNK // 2, NCHUNK):
        chunk(i)
    mcopy.wait()
    order_slots(meta, order)
    to_scalars = pltpu.make_async_copy(order, slots, in_sem.at[0])
    to_scalars.start()
    to_scalars.wait()
    for c in tcopies:
        c.wait_recv()

    def running(line, product, key, total, start, stop, halves):
        def step(q, total):
            for g in range(GROUP):
                k = q * GROUP + g
                entry = slots[line, k]
                before = slots[line, jnp.maximum(k - 1, 0)]
                fresh = key(entry) != key(before)
                total = jnp.where(fresh, 0.0, total) + product(
                    entry & (SLOTS - 1), (entry >> 8) & (RB - 1), (entry >> 12) & (NJB - 1)
                )
                for i, half in enumerate(halves):
                    cbuf[k, half] = total[:, i * TILE : (i + 1) * TILE].astype(bf16)
            return total

        return lax.fori_loop(start // GROUP, stop // GROUP, step, total)

    def to_workers(s, r, c):
        i = block_index(c)
        rows = jnp.concatenate([table[(0,) + i], table[(1,) + i]], axis=1)
        return jnp.dot(xbuf[s], rows, preferred_element_type=f32)

    def sum_jobs(half, workers):
        def to_jobs(s, r, c):
            return lax.dot_general(
                xbuf[s], workers[r], (((0,), (0,)), ((), ())), preferred_element_type=f32
            )

        total = jnp.zeros((TILE, TILE), f32)
        running(0, to_jobs, lambda entry: entry >> 12, total, 0, SLOTS, (0,))

        @pl.loop(0, NJB, unroll=4)
        def _(j):
            last = slots[2, j] & (SLOTS - 1)
            some = slots[3, j] > 0
            value = cbuf[last, 0]
            jobs[(half,) + block_index(j)] = jnp.where(some, value, jnp.zeros_like(value))

    hops = {}
    wave_lo = (x_lo, 1 - x_lo)

    def hop(p, stage, d, src, dst):
        target = shifted(at, REDUCE[p][2][stage], d)
        hops[p, stage, d] = remote(src, dst, ssend, srecv, p * 9 + stage * 3 + d - 1, target)

    def fixed_of(p, axis, by):
        fixed = labels_of(axis, (at[axis] + by) % 4)
        if REDUCE[p][3] is not None and axis != "x":
            fixed["x_lo"] = wave_lo[REDUCE[p][3]]
        return fixed

    def first_hop(p):
        rows = (slice(None), part_rows(REDUCE[p]), slice(None))
        for d in (2, 1, 3):
            fixed = fixed_of(p, REDUCE[p][2][0], d)
            hop(p, 0, d, jobs.at[index(LABELS, fixed) + rows], ra[p].at[d - 1])

    def first_sum(p, fixed):
        own = {**fixed_of(p, REDUCE[p][2][0], 0), **fixed}
        rows = (slice(None), part_rows(REDUCE[p]), slice(None))
        total = jobs[index(LABELS, own) + rows].astype(f32)
        for d in range(3):
            total += ra[p][(d,) + index(plan(REDUCE[p])[0], fixed)].astype(f32)
        return total

    def second_hop(p):
        after, _ = plan(REDUCE[p])
        for d in (1, 2, 3):
            hops[p, 0, d].wait_recv()
        count = 1
        for x in after:
            count *= LABELS[x]

        @pl.loop(0, count, unroll=4)
        def _(k):
            fixed = loop_labels(after, k)
            sa[p][index(after, fixed)] = first_sum(p, fixed).astype(bf16)

        for d in (2, 1, 3):
            a2 = REDUCE[p][2][1]
            fixed = labels_of(a2, (at[a2] + d) % 4)
            hop(p, 1, d, sa[p].at[index(after, fixed)], rb[p].at[d - 1])

    def third_hop(p):
        _, last = plan(REDUCE[p])
        _, _, (a1, a2, a3), wave = REDUCE[p]
        for d in (1, 2, 3):
            hops[p, 1, d].wait_recv()
        count = 1
        for x in last:
            count *= LABELS[x]

        @pl.loop(0, count, unroll=True)
        def _(k):
            fixed = loop_labels(last, k)
            total = first_sum(p, {**fixed, **labels_of(a2, at[a2])})
            for d in range(3):
                total += rb[p][(d,) + index(last, fixed)].astype(f32)
            sb[p][index(last, fixed)] = total

        for d in {None: (2, 1, 3), 0: (2,), 1: (1, 3)}[wave]:
            fixed = labels_of(a3, (at[a3] + d) % 4)
            hop(p, 2, d, sb[p].at[index(last, fixed)], rc[p].at[d - 1])

    def finish_sum(parts):
        p = parts[0]
        a3 = REDUCE[p][2][2]
        total = sb[p][index(plan(REDUCE[p])[1], labels_of(a3, at[a3]))]
        for q in parts:
            for d in (1, 2, 3):
                if (q, 2, d) in hops:
                    hops[q, 2, d].wait_recv()
                    total += rc[q][d - 1]
        jsum[:, part_rows(REDUCE[p]), :] = total

    sum_jobs(x_lo, wown)
    first_hop(0)
    first_hop(1)
    wcopy.wait()
    sum_jobs(1 - x_lo, wother)
    for p in (2, 3, 4):
        first_hop(p)
    for c in third.values():
        c.wait_recv()
    total = jnp.zeros((TILE, 2 * TILE), f32)
    row_of = lambda entry: (entry >> 8) & (RB - 1)
    total = running(1, to_workers, row_of, total, 0, SLOTS // 2, (0, 1))
    second_hop(0)
    second_hop(1)
    running(1, to_workers, row_of, total, SLOTS // 2, SLOTS, (0, 1))

    @pl.loop(0, RB)
    def _(j):
        last = slots[4, j] & (SLOTS - 1)
        some = slots[5, j] > 0
        for ref, half in ((away, 1 - x_lo), (kept, x_lo)):
            value = cbuf[last, half]
            ref[j] = jnp.where(some, value, jnp.zeros_like(value))

    acopy = remote(away, rw, osend, orecv, 2, x_mate)
    kcopy = pltpu.make_async_copy(kept, home, in_sem.at[0])
    kcopy.start()
    third_hop(0)
    third_hop(1)
    for p in (2, 3, 4):
        second_hop(p)
    for p in (2, 3, 4):
        third_hop(p)
    finish_sum((0, 2))
    finish_sum((1, 3))
    finish_sum((4,))
    kcopy.wait()
    acopy.wait()
    for copies in (first, second, third, hops):
        for c in copies.values():
            c.wait_send()
    for c in tcopies:
        c.wait_send()


def layer(wemb, wcot, jemb, jcot, wdeg, jdeg, brows, bcols, live, tiles):
    hbm = pl.BlockSpec(memory_space=pl.ANY)
    vmem = pl.BlockSpec(memory_space=pltpu.VMEM)
    ra, sa, rb, sb, rc = [], [], [], [], []
    for part in REDUCE:
        rows = (2, part[1], TILE)
        after, last = (tuple(LABELS[x] for x in labels) + rows for labels in plan(part))
        ra.append(pltpu.VMEM((3,) + after, jnp.bfloat16))
        sa.append(pltpu.VMEM(after, jnp.bfloat16))
        rb.append(pltpu.VMEM((3,) + last, jnp.bfloat16))
        sb.append(pltpu.VMEM(last, jnp.float32))
        rc.append(pltpu.VMEM((3,) + rows, jnp.float32))
    chunks = dims_of("xyz") + (2, TILE, TILE)
    dma = pltpu.SemaphoreType.DMA
    return pl.pallas_call(
        layer_kernel,
        in_specs=[hbm] * 4 + [vmem] * 5 + [hbm],
        out_specs=[hbm, hbm, vmem],
        out_shape=[
            jax.ShapeDtypeStruct((RB, TILE, TILE), jnp.bfloat16),
            jax.ShapeDtypeStruct((RB, TILE, TILE), jnp.bfloat16),
            jax.ShapeDtypeStruct((2, TILE, TILE), jnp.float32),
        ],
        scratch_shapes=[
            pltpu.VMEM((RB, TILE, TILE), jnp.bfloat16),
            pltpu.VMEM((RB, TILE, TILE), jnp.bfloat16),
            pltpu.VMEM((TILE, NW_LOC), jnp.float32),
            pltpu.VMEM((NBUF, TCHUNK, TILE, TILE), jnp.int32),
            pltpu.VMEM((SLOTS, TILE, TILE), jnp.bfloat16),
            pltpu.VMEM(chunks, jnp.bfloat16),
            pltpu.VMEM((TILE, JLOC), jnp.float32),
            pltpu.VMEM((2, 8, NB), jnp.int32),
            pltpu.VMEM((8, SLOTS), jnp.int32),
            pltpu.SMEM((8, SLOTS), jnp.int32),
            pltpu.VMEM((SLOTS, 2, TILE, TILE), jnp.bfloat16),
            pltpu.VMEM(chunks, jnp.bfloat16),
            pltpu.VMEM((RB, TILE, TILE), jnp.bfloat16),
            pltpu.VMEM((RB, TILE, TILE), jnp.bfloat16),
        ]
        + ra
        + sa
        + rb
        + sb
        + rc
        + [
            dma((4,)),
            dma((NBUF,)),
            dma((NCHUNK,)),
            dma((NCHUNK,)),
            dma((3,)),
            dma((3,)),
            dma((66,)),
            dma((66,)),
            dma((45,)),
            dma((45,)),
        ],
        compiler_params=pltpu.CompilerParams(
            collective_id=0, has_side_effects=True, vmem_limit_bytes=60 * 2**20
        ),
        name="layer",
    )(wemb, wcot, jemb, jcot, wdeg, jdeg, brows, bcols, live, tiles)


def finish_kernel(home, rw, jsum, wdeg, jdeg, wout, wgrad, jout, jgrad):
    def write(i, total, scale, out, grad):
        here = slice(i * TILE, (i + 1) * TILE)
        value = jnp.transpose(total) * scale[:, here]
        out[:, here] = value[:64]
        grad[:, here] = value[64:]

    scale = lax.rsqrt(wdeg[...].astype(jnp.float32))
    for i in range(RB):
        write(i, home[i].astype(jnp.float32) + rw[i].astype(jnp.float32), scale, wout, wgrad)
    scale = lax.rsqrt(jdeg[...].astype(jnp.float32))
    for i in range(2):
        write(i, jsum[i], scale, jout, jgrad)


def finish(home, rw, jsum, wdeg, jdeg):
    vmem = pl.BlockSpec(memory_space=pltpu.VMEM)
    return pl.pallas_call(
        finish_kernel,
        in_specs=[vmem] * 5,
        out_specs=[vmem] * 4,
        out_shape=[
            jax.ShapeDtypeStruct((64, NW_LOC), jnp.float32),
            jax.ShapeDtypeStruct((64, NW_LOC), jnp.float32),
            jax.ShapeDtypeStruct((64, JLOC), jnp.float32),
            jax.ShapeDtypeStruct((64, JLOC), jnp.float32),
        ],
        name="finish",
    )(home, rw, jsum, wdeg, jdeg)


def on_device(
    worker_emb,
    job_emb,
    worker_cot,
    job_cot,
    worker_deg,
    job_deg,
    block_rows,
    block_cols,
    block_tiles,
    live_count,
):
    wdeg, jdeg = worker_deg[None, :], job_deg[None, :]
    home, rw, jsum = layer(
        worker_emb.T,
        worker_cot.T,
        job_emb.T,
        job_cot.T,
        wdeg,
        jdeg,
        block_rows[None, :],
        block_cols[None, :],
        live_count,
        block_tiles,
    )
    worker_out, worker_grad, job_out, job_grad = finish(home, rw, jsum, wdeg, jdeg)
    return (worker_out.T, job_out.T, worker_grad.T, job_grad.T)


def solution(mesh):
    return jax.shard_map(
        on_device,
        mesh=mesh,
        in_specs=(
            P("blk", "col"),
            P("blk", "col"),
            P("blk", "col"),
            P("blk", "col"),
            P("blk"),
            P("blk"),
            P(("blk", "col")),
            P(("blk", "col")),
            P(("blk", "col"), None, None),
            P("blk", "col"),
        ),
        out_specs=(P("blk", "col"), P("blk", "col"), P("blk", "col"), P("blk", "col")),
        check_vma=False,
    )
```

time: 84.6 us -> 74.9 us (0.89)
  Pallas kernels: 83.1 us -> 73.3 us
    pallas_call x1, Pallas kernels: 80.5 us -> 70.8 us  [layer(): pl.pallas_call(layer_kernel, in_specs=[hbm] * 4 + [vmem] * 5 + [hbm], out...]
where the time goes in v3:
time: 74.9 us; the launch traced here: 74.6 us
  Pallas kernels  73.3 us (98%)
  between operations  1.29 us (2%)
    pallas_call x1, Pallas kernels, layer(): pl.pallas_call(layer_kernel, in_specs=[hbm] * 4 + [vmem] * 5 + [hbm], out...  70.8 us
    pallas_call x1, Pallas kernels, finish(): pl.pallas_call(finish_kernel, in_specs=[vmem] * 5, out_specs=[vmem] * 4,...  2.56 us

profile of v3, /device:TPU:0, one launch (start us, length us, event | category | flops | bytes accessed | tf_op | source)
XLA Modules:
  0.0 74.6 jit_solution(9266040308597226591)
XLA Ops:
  1.3 70.8 %layer.1 = (bf16[16,128,128]{2,1,0:T(8,128)(2,1)}, bf16[16,128,128]{2,1,0:T(8,128)(2,1)}, f32[2,128,128]{2,1,0:T(8,128)}) custom-call(f32[64,2048]{1,0:T(8,128)} %bitcast.12, f32[64,2048]{1,0:T(8,128)} %bitcast.13, f32[64,256]{1,0:T(8,128)} %bitcast.14, f32[64,256]{1,0:T(8,128)} %bitcast.15, s32[1,2048]{1,0:T(1,128)} %bitcast.16, s32[1,256]{1,0:T(1,128)} %bitcast.18, ...), custom_call_target="tpu_custom_call" | custom-call | tf_op jit(solution)/shard_map/layer/pallas_call | solution.py:473
  72.1 2.6 %finish.1 = (f32[64,2048]{1,0:T(8,128)}, f32[64,2048]{1,0:T(8,128)}, f32[64,256]{1,0:T(8,128)}, f32[64,256]{1,0:T(8,128)}) custom-call(bf16[16,128,128]{2,1,0:T(8,128)(2,1)} %get-tuple-element.11.home, bf16[16,128,128]{2,1,0:T(8,128)(2,1)} %get-tuple-element.12.rw, f32[2,128,128]{2,1,0:T(8,128)} %get-tuple-element.13.jsum, s32[1,2048]{1,0:T(1,128)} %bitcast.17, ...), custom_call_target="tpu_custom_call" | custom-call | tf_op jit(solution)/shard_map/finish/pallas_call | solution.py:539

commit v4 on v3

--- a/solution.py
+++ b/solution.py
@@ -26,7 +26,7 @@
 TCHUNK = 8
 NCHUNK = NB // TCHUNK
 NBUF = 4
-GROUP = 16
+GROUP = 32
 SLOTS = 2 * NB
 
 
@@ -238,6 +238,11 @@
         table[pick("xyz", at) + (i,)] = jnp.transpose(
             rows_in[:, here] * job_scale[:, here]
         ).astype(bf16)
+    ins[2].wait()
+    ins[3].wait()
+    for i in range(RB):
+        here = slice(i * TILE, (i + 1) * TILE)
+        wown[i] = jnp.transpose(dense_in[:, here] * worker_scale[:, here]).astype(bf16)
     pl.semaphore_wait(barrier, len(others))
     first, second, third = {}, {}, {}
     for d in (1, 3, 2):
@@ -247,11 +252,6 @@
                 own, own, gsend, grecv, p * 22 + d - 1, shifted(at, SPREAD[p][2][0], d)
             )
     mcopy = remote(meta.at[core], meta.at[core], osend, orecv, 0, core_mate)
-    ins[2].wait()
-    ins[3].wait()
-    for i in range(RB):
-        here = slice(i * TILE, (i + 1) * TILE)
-        wown[i] = jnp.transpose(dense_in[:, here] * worker_scale[:, here]).astype(bf16)
     wcopy = remote(wown, wother, osend, orecv, 1, x_mate)
 
     tcopies = []
@@ -416,7 +416,7 @@
     first_hop(1)
     wcopy.wait()
     sum_jobs(1 - x_lo, wother)
-    for p in (2, 3, 4):
+    for p in (4, 2, 3):
         first_hop(p)
     for c in third.values():
         c.wait_recv()
@@ -438,11 +438,9 @@
     acopy = remote(away, rw, osend, orecv, 2, x_mate)
     kcopy = pltpu.make_async_copy(kept, home, in_sem.at[0])
     kcopy.start()
-    third_hop(0)
-    third_hop(1)
-    for p in (2, 3, 4):
+    for p in (4, 2, 3):
         second_hop(p)
-    for p in (2, 3, 4):
+    for p in (0, 1, 4, 2, 3):
         third_hop(p)
     finish_sum((0, 2))
     finish_sum((1, 3))

time: 74.9 us -> 74.3 us (level)
  no operation moved by 1% of the time
where the time goes in v4:
time: 74.3 us; the launch traced here: 74.1 us
  Pallas kernels  72.8 us (98%)
  between operations  1.29 us (2%)
    pallas_call x1, Pallas kernels, layer(): pl.pallas_call(layer_kernel, in_specs=[hbm] * 4 + [vmem] * 5 + [hbm], out...  70.2 us
    pallas_call x1, Pallas kernels, finish(): pl.pallas_call(finish_kernel, in_specs=[vmem] * 5, out_specs=[vmem] * 4,...  2.56 us

profile of v4, /device:TPU:0, one launch (start us, length us, event | category | flops | bytes accessed | tf_op | source)
XLA Modules:
  0.0 74.1 jit_solution(1029620092330839394)
XLA Ops:
  1.3 70.2 %layer.1 = (bf16[16,128,128]{2,1,0:T(8,128)(2,1)}, bf16[16,128,128]{2,1,0:T(8,128)(2,1)}, f32[2,128,128]{2,1,0:T(8,128)}) custom-call(f32[64,2048]{1,0:T(8,128)} %bitcast.12, f32[64,2048]{1,0:T(8,128)} %bitcast.13, f32[64,256]{1,0:T(8,128)} %bitcast.14, f32[64,256]{1,0:T(8,128)} %bitcast.15, s32[1,2048]{1,0:T(1,128)} %bitcast.16, s32[1,256]{1,0:T(1,128)} %bitcast.18, ...), custom_call_target="tpu_custom_call" | custom-call | tf_op jit(solution)/shard_map/layer/pallas_call | solution.py:471
  71.5 2.6 %finish.1 = (f32[64,2048]{1,0:T(8,128)}, f32[64,2048]{1,0:T(8,128)}, f32[64,256]{1,0:T(8,128)}, f32[64,256]{1,0:T(8,128)}) custom-call(bf16[16,128,128]{2,1,0:T(8,128)(2,1)} %get-tuple-element.11.home, bf16[16,128,128]{2,1,0:T(8,128)(2,1)} %get-tuple-element.12.rw, f32[2,128,128]{2,1,0:T(8,128)} %get-tuple-element.13.jsum, s32[1,2048]{1,0:T(1,128)} %bitcast.17, ...), custom_call_target="tpu_custom_call" | custom-call | tf_op jit(solution)/shard_map/finish/pallas_call | solution.py:537

commit v5 on v3

--- a/solution.py
+++ b/solution.py
@@ -26,7 +26,7 @@
 TCHUNK = 8
 NCHUNK = NB // TCHUNK
 NBUF = 4
-GROUP = 16
+GROUP = 32
 SLOTS = 2 * NB
 
 
@@ -105,6 +105,13 @@
         fixed[x] = k % LABELS[x]
         k = k // LABELS[x]
     return fixed
+
+
+def chunks_of(labels):
+    count = 1
+    for x in labels:
+        count *= LABELS[x]
+    return count
 
 
 def block_index(j):
@@ -183,8 +190,9 @@
     kept,
     *rest,
 ):
-    ra, sa, rb, sb, rc = (rest[i : i + len(REDUCE)] for i in range(0, 5 * len(REDUCE), len(REDUCE)))
-    in_sem, tin_sem, tsend, trecv, osend, orecv, gsend, grecv, ssend, srecv = rest[5 * len(REDUCE) :]
+    n = len(REDUCE)
+    ra, fs, sa, rb, sb, rc = (rest[i : i + n] for i in range(0, 6 * n, n))
+    in_sem, tin_sem, tsend, trecv, osend, orecv, gsend, grecv, ssend, srecv = rest[6 * n :]
     at = position()
     x_lo = at["x"] % 2
     core = at["core"]
@@ -337,9 +345,9 @@
     hops = {}
     wave_lo = (x_lo, 1 - x_lo)
 
-    def hop(p, stage, d, src, dst):
+    def hop(p, name, stage, d, sem, src, dst):
         target = shifted(at, REDUCE[p][2][stage], d)
-        hops[p, stage, d] = remote(src, dst, ssend, srecv, p * 9 + stage * 3 + d - 1, target)
+        hops[p, name] = remote(src, dst, ssend, srecv, p * 12 + sem, target)
 
     def fixed_of(p, axis, by):
         fixed = labels_of(axis, (at[axis] + by) % 4)
@@ -347,29 +355,54 @@
             fixed["x_lo"] = wave_lo[REDUCE[p][3]]
         return fixed
 
+    def halves_of(p, d):
+        fixed = fixed_of(p, REDUCE[p][2][0], d)
+        rows = part_rows(REDUCE[p])
+        return [jobs.at[index(LABELS, fixed) + (half, rows, slice(None))] for half in (0, 1)]
+
+    def slot_half(ref, p, half):
+        return ref.at[index(plan(REDUCE[p])[0], {}) + (half,)]
+
     def first_hop(p):
-        rows = (slice(None), part_rows(REDUCE[p]), slice(None))
-        for d in (2, 1, 3):
-            fixed = fixed_of(p, REDUCE[p][2][0], d)
-            hop(p, 0, d, jobs.at[index(LABELS, fixed) + rows], ra[p].at[d - 1])
+        far, right, left = halves_of(p, 2), halves_of(p, 1), halves_of(p, 3)
+        hop(p, "far_r", 0, 1, 0, far[0], slot_half(ra[p].at[2], p, 0))
+        hop(p, "far_l", 0, 3, 1, far[1], slot_half(ra[p].at[2], p, 1))
+        hop(p, "right", 0, 1, 2, right[1], slot_half(ra[p].at[0], p, 1))
+        hop(p, "left", 0, 3, 3, left[0], slot_half(ra[p].at[1], p, 0))
+
+    def add_far(p):
+        a1 = REDUCE[p][2][0]
+        after, _ = plan(REDUCE[p])
+        hops[p, "far_r"].wait_recv()
+        hops[p, "far_l"].wait_recv()
+
+        @pl.loop(0, chunks_of(after), unroll=4)
+        def _(k):
+            fixed = loop_labels(after, k)
+            for half, d in ((0, 1), (1, 3)):
+                theirs = {**fixed_of(p, a1, d), **fixed}
+                here = index(LABELS, theirs) + (half, part_rows(REDUCE[p]), slice(None))
+                place = index(after, fixed) + (half,)
+                total = jobs[here].astype(f32) + ra[p][(2,) + place].astype(f32)
+                fs[p][place] = total.astype(bf16)
+
+        hop(p, "sum_r", 0, 1, 4, slot_half(fs[p], p, 0), slot_half(ra[p].at[0], p, 0))
+        hop(p, "sum_l", 0, 3, 5, slot_half(fs[p], p, 1), slot_half(ra[p].at[1], p, 1))
 
     def first_sum(p, fixed):
         own = {**fixed_of(p, REDUCE[p][2][0], 0), **fixed}
         rows = (slice(None), part_rows(REDUCE[p]), slice(None))
         total = jobs[index(LABELS, own) + rows].astype(f32)
-        for d in range(3):
-            total += ra[p][(d,) + index(plan(REDUCE[p])[0], fixed)].astype(f32)
+        for slot in range(2):
+            total += ra[p][(slot,) + index(plan(REDUCE[p])[0], fixed)].astype(f32)
         return total
 
     def second_hop(p):
         after, _ = plan(REDUCE[p])
-        for d in (1, 2, 3):
-            hops[p, 0, d].wait_recv()
-        count = 1
-        for x in after:
-            count *= LABELS[x]
-
-        @pl.loop(0, count, unroll=4)
+        for name in ("right", "left", "sum_r", "sum_l"):
+            hops[p, name].wait_recv()
+
+        @pl.loop(0, chunks_of(after), unroll=4)
         def _(k):
             fixed = loop_labels(after, k)
             sa[p][index(after, fixed)] = first_sum(p, fixed).astype(bf16)
@@ -377,18 +410,15 @@
         for d in (2, 1, 3):
             a2 = REDUCE[p][2][1]
             fixed = labels_of(a2, (at[a2] + d) % 4)
-            hop(p, 1, d, sa[p].at[index(after, fixed)], rb[p].at[d - 1])
+            hop(p, (1, d), 1, d, 5 + d, sa[p].at[index(after, fixed)], rb[p].at[d - 1])
 
     def third_hop(p):
         _, last = plan(REDUCE[p])
         _, _, (a1, a2, a3), wave = REDUCE[p]
         for d in (1, 2, 3):
-            hops[p, 1, d].wait_recv()
-        count = 1
-        for x in last:
-            count *= LABELS[x]
-
-        @pl.loop(0, count, unroll=True)
+            hops[p, (1, d)].wait_recv()
+
+        @pl.loop(0, chunks_of(last), unroll=True)
         def _(k):
             fixed = loop_labels(last, k)
             total = first_sum(p, {**fixed, **labels_of(a2, at[a2])})
@@ -398,7 +428,7 @@
 
         for d in {None: (2, 1, 3), 0: (2,), 1: (1, 3)}[wave]:
             fixed = labels_of(a3, (at[a3] + d) % 4)
-            hop(p, 2, d, sb[p].at[index(last, fixed)], rc[p].at[d - 1])
+            hop(p, (2, d), 2, d, 8 + d, sb[p].at[index(last, fixed)], rc[p].at[d - 1])
 
     def finish_sum(parts):
         p = parts[0]
@@ -406,8 +436,8 @@
         total = sb[p][index(plan(REDUCE[p])[1], labels_of(a3, at[a3]))]
         for q in parts:
             for d in (1, 2, 3):
-                if (q, 2, d) in hops:
-                    hops[q, 2, d].wait_recv()
+                if (q, (2, d)) in hops:
+                    hops[q, (2, d)].wait_recv()
                     total += rc[q][d - 1]
         jsum[:, part_rows(REDUCE[p]), :] = total
 
@@ -418,13 +448,15 @@
     sum_jobs(1 - x_lo, wother)
     for p in (2, 3, 4):
         first_hop(p)
+    add_far(0)
+    add_far(1)
     for c in third.values():
         c.wait_recv()
     total = jnp.zeros((TILE, 2 * TILE), f32)
     row_of = lambda entry: (entry >> 8) & (RB - 1)
     total = running(1, to_workers, row_of, total, 0, SLOTS // 2, (0, 1))
-    second_hop(0)
-    second_hop(1)
+    for p in (2, 3, 4):
+        add_far(p)
     running(1, to_workers, row_of, total, SLOTS // 2, SLOTS, (0, 1))
 
     @pl.loop(0, RB)
@@ -438,11 +470,9 @@
     acopy = remote(away, rw, osend, orecv, 2, x_mate)
     kcopy = pltpu.make_async_copy(kept, home, in_sem.at[0])
     kcopy.start()
-    third_hop(0)
-    third_hop(1)
-    for p in (2, 3, 4):
+    for p in range(len(REDUCE)):
         second_hop(p)
-    for p in (2, 3, 4):
+    for p in range(len(REDUCE)):
         third_hop(p)
     finish_sum((0, 2))
     finish_sum((1, 3))
@@ -459,11 +489,12 @@
 def layer(wemb, wcot, jemb, jcot, wdeg, jdeg, brows, bcols, live, tiles):
     hbm = pl.BlockSpec(memory_space=pl.ANY)
     vmem = pl.BlockSpec(memory_space=pltpu.VMEM)
-    ra, sa, rb, sb, rc = [], [], [], [], []
+    ra, fs, sa, rb, sb, rc = [], [], [], [], [], []
     for part in REDUCE:
         rows = (2, part[1], TILE)
         after, last = (tuple(LABELS[x] for x in labels) + rows for labels in plan(part))
         ra.append(pltpu.VMEM((3,) + after, jnp.bfloat16))
+        fs.append(pltpu.VMEM(after, jnp.bfloat16))
         sa.append(pltpu.VMEM(after, jnp.bfloat16))
         rb.append(pltpu.VMEM((3,) + last, jnp.bfloat16))
         sb.append(pltpu.VMEM(last, jnp.float32))
@@ -496,6 +527,7 @@
             pltpu.VMEM((RB, TILE, TILE), jnp.bfloat16),
         ]
         + ra
+        + fs
         + sa
         + rb
         + sb
@@ -509,8 +541,8 @@
             dma((3,)),
             dma((66,)),
             dma((66,)),
-            dma((45,)),
-            dma((45,)),
+            dma((60,)),
+            dma((60,)),
         ],
         compiler_params=pltpu.CompilerParams(
             collective_id=0, has_side_effects=True, vmem_limit_bytes=60 * 2**20

time: 74.9 us -> 71.8 us (0.959)
  Pallas kernels: 73.3 us -> 70.3 us
    pallas_call x1, Pallas kernels: 70.8 us -> 67.7 us  [layer(): pl.pallas_call(layer_kernel, in_specs=[hbm] * 4 + [vmem] * 5 + [hbm], out...]
where the time goes in v5:
time: 71.8 us; the launch traced here: 71.5 us
  Pallas kernels  70.3 us (98%)
  between operations  1.29 us (2%)
    pallas_call x1, Pallas kernels, layer(): pl.pallas_call(layer_kernel, in_specs=[hbm] * 4 + [vmem] * 5 + [hbm], out...  67.7 us
    pallas_call x1, Pallas kernels, finish(): pl.pallas_call(finish_kernel, in_specs=[vmem] * 5, out_specs=[vmem] * 4,...  2.56 us

profile of v5, /device:TPU:0, one launch (start us, length us, event | category | flops | bytes accessed | tf_op | source)
XLA Modules:
  0.0 71.5 jit_solution(14541984532790736659)
XLA Ops:
  1.3 67.7 %layer.1 = (bf16[16,128,128]{2,1,0:T(8,128)(2,1)}, bf16[16,128,128]{2,1,0:T(8,128)(2,1)}, f32[2,128,128]{2,1,0:T(8,128)}) custom-call(f32[64,2048]{1,0:T(8,128)} %bitcast.12, f32[64,2048]{1,0:T(8,128)} %bitcast.13, f32[64,256]{1,0:T(8,128)} %bitcast.14, f32[64,256]{1,0:T(8,128)} %bitcast.15, s32[1,2048]{1,0:T(1,128)} %bitcast.16, s32[1,256]{1,0:T(1,128)} %bitcast.18, ...), custom_call_target="tpu_custom_call" | custom-call | tf_op jit(solution)/shard_map/layer/pallas_call | solution.py:504
  69.0 2.6 %finish.1 = (f32[64,2048]{1,0:T(8,128)}, f32[64,2048]{1,0:T(8,128)}, f32[64,256]{1,0:T(8,128)}, f32[64,256]{1,0:T(8,128)}) custom-call(bf16[16,128,128]{2,1,0:T(8,128)(2,1)} %get-tuple-element.11.home, bf16[16,128,128]{2,1,0:T(8,128)(2,1)} %get-tuple-element.12.rw, f32[2,128,128]{2,1,0:T(8,128)} %get-tuple-element.13.jsum, s32[1,2048]{1,0:T(1,128)} %bitcast.17, ...), custom_call_target="tpu_custom_call" | custom-call | tf_op jit(solution)/shard_map/finish/pallas_call | solution.py:571
